TPU v7x, 32 devices: a whole 2x2x4 slice. The times are simulated.
32 devices in a mesh: expert: 8 (over z, y), context: 4 (over x, core).
Axes of the slice: x: 2, y: 2, z: 4, core: 2. Of those that a mesh axis runs over, the one named last changes fastest.
Arguments:
- tokens: bfloat16 [8, 512, 2048], P('expert', 'context'), may hold values from -6 to 6
- route: int32 [8, 512, 1], P('expert'), may hold values from 0 to 7; in each aligned block of 128 rows (0 to 127, 128 to 255, ..., all dimensions but the last counted through in order) at most 32 rows name the same one
- w_inner: bfloat16 [8, 2048, 2, 4096], P('expert', None, None, 'context'), may hold values from -0.125 to 0.125
- w_state: bfloat16 [8, 2048, 128], P('expert'), may hold values from -0.015625 to 0.015625
- w_step: bfloat16 [8, 2048, 64], P('expert', None, 'context'), may hold values from -0.125 to 0.125
- step_bias: float32 [64], P('context'), may hold values from -2 to 0.5
- decay_log: float32 [64], P('context'), may hold values from -7 to -2.5
- skip_gain: float32 [64], P('context'), may hold values from 0.5 to 1.5
- conv_weight: float32 [4, 4096], P(None, 'context'), may hold values from -3 to 3
- conv_bias: float32 [4096], P('context'), may hold values from -1.5 to 1.5
- w_out: bfloat16 [8, 4096, 2048], P('expert', 'context'), may hold values from -0.09375 to 0.09375
Outputs:
- mixed: bfloat16 [8, 512, 2048], P('expert', 'context')
Inputs may be any that keep to these rules, and one draw needn't show every extreme that they name: `route`: in each aligned block of 128 positions (the rows of one device) no expert is named more than 32 times, a bound that some block reaches.
All inputs are finite; a program needn't handle non-finite values.
Results may differ from a plain program's by a relative error of at most 0.014.
Values may be sent and summed in bfloat16 or wider, within the bound.
No kernel may reach another device: no remote copies, remote signals or barrier semaphores. Data moves between devices by JAX's collectives and lax.ppermute only.
A program may use at most 128 MiB of HBM per device.

v0:
```python
import math

import jax
import jax.numpy as jnp
from jax import lax
from jax.sharding import PartitionSpec as P

HEAD_DIM = 64


def block_ranks(ids_flat, experts, tok_rows):
    blocks = ids_flat.reshape(-1, tok_rows)
    onehot = (blocks[:, :, None] == jnp.arange(experts, dtype=jnp.int32)[None, None, :]).astype(
        jnp.int32
    )
    before = jnp.cumsum(onehot, axis=1) - 1
    return jnp.sum(onehot * before, axis=2)


def causal_conv(values, conv_weight, conv_bias):
    taps = conv_weight.shape[0]
    length = values.shape[0]
    padded = jnp.pad(values, ((taps - 1, 0), (0, 0)))
    total = conv_bias[None, :] + jnp.zeros_like(values)
    for shift in range(taps):
        total = total + conv_weight[shift][None, :] * padded[shift : shift + length]
    return total


def state_scan(signal_heads, steps, rates, in_vecs, out_vecs):
    length, heads, head_dim = signal_heads.shape
    nstate = in_vecs.shape[1]
    block = math.gcd(length, 128)
    count = length // block
    exact = lax.Precision.HIGHEST
    logs = steps * rates[None, :]
    pieces = (
        signal_heads.reshape(count, block, heads, head_dim),
        steps.reshape(count, block, heads),
        logs.reshape(count, block, heads),
        in_vecs.reshape(count, block, nstate),
        out_vecs.reshape(count, block, nstate),
    )
    lower = jnp.arange(block)[:, None] >= jnp.arange(block)[None, :]

    def advance(state, piece):
        values, step_now, log_now, keys, queries = piece
        summed = jnp.cumsum(log_now, axis=0)
        gaps = summed[:, None, :] - summed[None, :, :]
        decay = jnp.exp(jnp.where(lower[:, :, None], gaps, -jnp.inf))
        scores = jnp.dot(queries, keys.T, precision=exact)
        weights = scores[:, :, None] * decay * step_now[None, :, :]
        local = jnp.einsum("tuh,uhp->thp", weights, values, precision=exact)
        carried = jnp.exp(summed)[:, :, None] * jnp.einsum(
            "tn,hpn->thp", queries, state, precision=exact
        )
        tail = jnp.exp(summed[-1][None, :] - summed) * step_now
        state = jnp.exp(summed[-1])[:, None, None] * state + jnp.einsum(
            "uh,uhp,un->hpn", tail, values, keys, precision=exact
        )
        return (state, local + carried)

    start = jnp.zeros((heads, head_dim, nstate), jnp.float32)
    final_state, outputs = lax.scan(advance, start, pieces)
    return outputs.reshape(length, heads, head_dim)


def mix_sequence(
    gate_inner,
    state_in_out,
    step_raw,
    conv_weight,
    conv_bias,
    step_bias,
    decay_log,
    skip_gain,
    head_dim,
):
    length = gate_inner.shape[0]
    gate_part = gate_inner[:, 0].astype(jnp.float32)
    inner_part = gate_inner[:, 1].astype(jnp.float32)
    signal = jax.nn.silu(causal_conv(inner_part, conv_weight, conv_bias))
    heads = step_raw.shape[1]
    steps = jax.nn.softplus(step_raw.astype(jnp.float32) + step_bias[None, :])
    rates = -jnp.exp(decay_log)
    nstate = state_in_out.shape[1] // 2
    in_vecs = state_in_out[:, :nstate].astype(jnp.float32)
    out_vecs = state_in_out[:, nstate:].astype(jnp.float32)
    signal_heads = signal.reshape(length, heads, head_dim)
    scanned = state_scan(signal_heads, steps, rates, in_vecs, out_vecs)
    scanned = scanned + skip_gain[None, :, None] * signal_heads
    return (scanned.reshape(length, heads * head_dim) * jax.nn.silu(gate_part)).astype(jnp.bfloat16)


def per_device(
    tokens,
    route,
    w_inner,
    w_state,
    w_step,
    step_bias,
    decay_log,
    skip_gain,
    conv_weight,
    conv_bias,
    w_out,
):
    tok_rows = tokens.shape[1]
    width = tokens.shape[2]
    experts = lax.axis_size("expert")
    shards = lax.axis_size("context")
    capacity = 2 * tok_rows // experts
    chans = w_inner.shape[3]
    length = route.shape[1]
    ids_seq = route[0, :, 0]
    ranks = block_ranks(ids_seq, experts, tok_rows)
    here = lax.axis_index("context")
    mine_ids = lax.dynamic_slice_in_dim(ids_seq, here * tok_rows, tok_rows)
    mine_ranks = lax.dynamic_index_in_dim(ranks, here, 0, keepdims=False)
    local_slot = mine_ids * capacity + mine_ranks
    dispatch = (
        local_slot[None, :] == jnp.arange(experts * capacity, dtype=jnp.int32)[:, None]
    ).astype(jnp.bfloat16)
    outgoing = jnp.dot(dispatch, tokens[0], preferred_element_type=jnp.float32).astype(jnp.bfloat16)
    outgoing = outgoing.reshape(experts, capacity, width)
    arrived = lax.all_to_all(outgoing, "expert", split_axis=0, concat_axis=0, tiled=True)
    gathered = lax.all_gather(arrived, "context", axis=1, tiled=True)
    rows = gathered.reshape(-1, width)
    gate_inner = jnp.dot(
        rows, w_inner[0].reshape(width, 2 * chans), preferred_element_type=jnp.float32
    ).astype(jnp.bfloat16)
    state_part = jnp.dot(rows, w_state[0], preferred_element_type=jnp.float32).astype(jnp.bfloat16)
    step_part = jnp.dot(rows, w_step[0], preferred_element_type=jnp.float32).astype(jnp.bfloat16)
    gate_inner = gate_inner.reshape(experts, shards * capacity, 2 * chans)
    state_part = state_part.reshape(experts, shards * capacity, state_part.shape[1])
    step_part = step_part.reshape(experts, shards * capacity, step_part.shape[1])
    gate_back, state_back, step_back = (
        lax.all_to_all(gate_inner, "expert", split_axis=0, concat_axis=0, tiled=True),
        lax.all_to_all(state_part, "expert", split_axis=0, concat_axis=0, tiled=True),
        lax.all_to_all(step_part, "expert", split_axis=0, concat_axis=0, tiled=True),
    )
    seq_slot = (
        (ids_seq.reshape(shards, tok_rows) * shards + jnp.arange(shards, dtype=jnp.int32)[:, None])
        * capacity
        + ranks
    ).reshape(length)
    seq_gate = jnp.take(gate_back.reshape(-1, 2 * chans), seq_slot, axis=0).reshape(
        length, 2, chans
    )
    seq_state = jnp.take(state_back.reshape(-1, state_back.shape[2]), seq_slot, axis=0)
    seq_step = jnp.take(step_back.reshape(-1, step_back.shape[2]), seq_slot, axis=0)
    gated = mix_sequence(
        seq_gate,
        seq_state,
        seq_step,
        conv_weight,
        conv_bias,
        step_bias,
        decay_log,
        skip_gain,
        HEAD_DIM,
    )
    owner = (
        jnp.full((experts * shards * capacity,), length, jnp.int32)
        .at[seq_slot]
        .set(jnp.arange(length, dtype=jnp.int32))
    )
    leaving = jnp.take(gated, owner, axis=0, mode="fill", fill_value=0).reshape(
        experts, shards * capacity, chans
    )
    returned = lax.all_to_all(leaving, "expert", split_axis=0, concat_axis=0, tiled=True)
    parts = jnp.dot(
        returned.reshape(-1, chans), w_out[0], preferred_element_type=jnp.float32
    ).astype(jnp.bfloat16)
    parts = parts.reshape(experts, shards, capacity, width)
    pieces = lax.all_to_all(
        lax.all_to_all(parts, "expert", split_axis=0, concat_axis=0, tiled=True),
        "context",
        split_axis=1,
        concat_axis=1,
        tiled=True,
    )
    summed = jnp.sum(pieces.astype(jnp.float32), axis=1).astype(jnp.bfloat16)
    result = jnp.take(summed.reshape(-1, width), local_slot, axis=0)
    return result[None]


def solution(mesh):
    in_specs = (
        P("expert", "context", None),
        P("expert", None, None),
        P("expert", None, None, "context"),
        P("expert", None, None),
        P("expert", None, "context"),
        P("context"),
        P("context"),
        P("context"),
        P(None, "context"),
        P("context"),
        P("expert", "context", None),
    )
    out_specs = P("expert", "context", None)
    return jax.shard_map(
        per_device, mesh=mesh, in_specs=in_specs, out_specs=out_specs, check_vma=False
    )
```

profile of v0, /device:TPU:0, one launch (start us, length us, event | category | flops | bytes accessed | tf_op | source)
XLA Modules:
  0.0 500.1 jit_solution(14903890120652826255)
XLA Ops:
  9.7 33.0 %all_to_all.35 = bf16[8,32,2048]{2,1,0:T(8,128)(2,1)} all-to-all(bf16[8,32,2048]{2,1,0:T(8,128)(2,1)S(1)} %bitcast.187), channel_id=1, replica_groups=mesh['expert'=8,'context'=4] {'expert'}, dimensions={0} | all-to-all | bytes 2097152 | tf_op jit(solution)/shard_map/all_to_all | solution.py:126
  42.7 10.4 %copy.113 = bf16[256,8,2,1024]{3,1,2,0:T(8,128)(2,1)} copy(bf16[256,8,2,1024]{3,2,1,0:T(2,128)(2,1)} %bitcast.177) | data formatting | bytes 16777216
  53.1 23.2 %all-gather.2.cloned.1.call-done = bf16[8,128,2048]{2,1,0:T(8,128)(2,1)} async-done(((bf16[8,32,2048]{2,1,0:T(8,128)(2,1)}), bf16[8,128,2048]{2,1,0:T(8,128)(2,1)}) %all-gather.2.cloned.1.call-update) | async-done | bytes 4194320 | tf_op jit(solution)/shard_map/all_gather | solution.py:127
  80.4 5.5 %all-to-all-start.1 = ((bf16[8,128,16]{1,2,0:T(8,128)(2,1)}), bf16[8,128,16]{1,2,0:T(8,128)(2,1)S(1)}, u32[]{:S(2)}, u32[]{:S(2)}) async-start(bf16[8,128,16]{1,2,0:T(8,128)(2,1)} %bitcast.149), calls=%async_computation.1 | async-start | bytes 65536 | tf_op jit(solution)/shard_map/all_to_all | solution.py:140
  85.9 4.1 convolution_convert_fusion.2
  96.0 13.8 %convolution_convert_fusion = bf16[1024,2048]{1,0:T(8,128)(2,1)} fusion(bf16[1024,2048]{1,0:T(8,128)(2,1)} %bitcast.184, bf16[2048,2048]{1,0:T(8,128)(2,1)} %bitcast.178), kind=kOutput, calls=%fused_computation.55 | convolution fusion | flops 8592031744 | bytes 16777216 | tf_op jit(solution)/shard_map/dot_general | solution.py:129
  109.9 6.1 %all-to-all-start.2 = ((bf16[8,128,2048]{2,1,0:T(8,128)(2,1)}), bf16[8,128,2048]{2,1,0:T(8,128)(2,1)}, u32[]{:S(2)}, u32[]{:S(2)}) async-start(bf16[8,128,2048]{2,1,0:T(8,128)(2,1)} %bitcast.185), calls=%async_computation.2 | async-start | bytes 8388608 | tf_op jit(solution)/shard_map/all_to_all | solution.py:138
  122.5 86.1 %all-to-all-done.2 = bf16[8,128,2048]{2,1,0:T(8,128)(2,1)} async-done(((bf16[8,128,2048]{2,1,0:T(8,128)(2,1)}), bf16[8,128,2048]{2,1,0:T(8,128)(2,1)}, u32[]{:S(2)}, u32[]{:S(2)}) %all-to-all-start.2) | async-done | bytes 4194336 | tf_op jit(solution)/shard_map/all_to_all | solution.py:138
  208.6 7.1 %gather_fusion.1 = bf16[512,2048]{1,0:T(8,128)(2,1)S(1)} fusion(bf16[1024,2048]{1,0:T(8,128)(2,1)} %bitcast.21, s32[1024]{0:T(1024)S(1)} %pad_clamp_fusion.1), kind=kCustom, calls=%fused_computation.1 | custom fusion | bytes 4196352 | tf_op jit(solution)/shard_map/jit(_take)/gather | solution.py:147
  220.7 4.5 reshape.328
  225.2 4.1 copy.96
  229.3 33.8 %while.13 = (s32[]{:T(128)}, f32[16,64,64]{2,1,0:T(8,128)S(1)}, f32[4,128,16,64]{1,3,2,0:T(8,128)}, f32[4,128,16]{1,2,0:T(8,128)S(1)}, f32[4,128,16]{1,2,0:T(8,1...) while((s32[]{:T(128)}, f32[16,64,64]{2,1,0:T(8,128)S(1)}, ...), condition=%wide.region_5.6_spmd.clone, body=%wide.region_3.5_spmd.clone.sunk | while | flops 417220608 | bytes 4435908 | solution.py:64
  231.5 4.3 fusion.95
  240.0 4.2 fusion.95
  248.4 4.2 fusion.95
  256.9 4.2 fusion.95
  263.1 4.0 copy.106
  267.1 4.9 reshape.329
  275.4 4.1 gather_fusion.3
  279.7 52.1 %all_to_all.36 = bf16[8,128,1024]{2,1,0:T(8,128)(2,1)S(1)} all-to-all(bf16[8,128,1024]{2,1,0:T(8,128)(2,1)S(1)} %broadcast_select_fusion), channel_id=1, replica_groups=mesh['expert'=8,'context'=4] {'expert'}, dimensions={0} | all-to-all | bytes 4194304 | tf_op jit(solution)/shard_map/all_to_all | solution.py:171
  331.8 4.7 fusion.41
  336.5 96.5 %all_to_all.37 = bf16[8,4,32,2048]{3,2,1,0:T(8,128)(2,1)S(1)} all-to-all(bf16[8,4,32,2048]{3,2,1,0:T(8,128)(2,1)S(1)} %bitcast.186), channel_id=1, replica_groups=mesh['expert'=8,'context'=4] {'expert'}, dimensions={0} | all-to-all | bytes 8388608 | tf_op jit(solution)/shard_map/all_to_all | solution.py:177
  435.2 4.8 all-to-all-start.6
  440.1 48.2 %all-to-all-done.6 = bf16[8,4,32,2048]{3,2,0,1:T(8,128)(2,1)} async-done(((bf16[8,4,32,2048]{3,2,0,1:T(8,128)(2,1)}), bf16[8,4,32,2048]{3,2,0,1:T(8,128)(2,1)}, u32[]{:S(2)}, u32[]{:S(2)}) %all-to-all-start.6) | async-done | bytes 4194336 | tf_op jit(solution)/shard_map/all_to_all | solution.py:176
  (129 shorter events, 52.0 us)
Async XLA Ops:
  6.5 2.7 copy-start
  6.5 69.8 %all-gather.2.cloned.1.call-start = ((), (), s32[]{:S(2)}) async-start(), calls=%async_computation.7 | async-start | bytes 5242880 | tf_op jit(solution)/shard_map/all_gather | solution.py:127
  42.7 33.6 %copy-start.4 = (bf16[1,2048,16]{1,2,0:T(8,128)(2,1)S(1)}, bf16[1,2048,16]{1,2,0:T(8,128)(2,1)}, u32[]{:S(2)}) copy-start(bf16[1,2048,16]{1,2,0:T(8,128)(2,1)} %param.17) | copy-start | bytes 196612
  76.3 9.6 %copy-start.10 = (bf16[1,2048,128]{2,1,0:T(8,128)(2,1)S(1)}, bf16[1,2048,128]{2,1,0:T(8,128)(2,1)}, u32[]{:S(2)}) copy-start(bf16[1,2048,128]{2,1,0:T(8,128)(2,1)} %param.16) | copy-start | bytes 1572868
  80.4 12.2 %all-to-all-start.1 = ((bf16[8,128,16]{1,2,0:T(8,128)(2,1)}), bf16[8,128,16]{1,2,0:T(8,128)(2,1)S(1)}, u32[]{:S(2)}, u32[]{:S(2)}) async-start(bf16[8,128,16]{1,2,0:T(8,128)(2,1)} %bitcast.149), calls=%async_computation.1 | async-start | bytes 65536 | tf_op jit(solution)/shard_map/all_to_all | solution.py:140
  92.6 17.3 %all-to-all-start.3 = ((bf16[8,128,128]{2,1,0:T(8,128)(2,1)}), bf16[8,128,128]{2,1,0:T(8,128)(2,1)S(1)}, u32[]{:S(2)}, u32[]{:S(2)}) async-start(bf16[8,128,128]{2,1,0:T(8,128)(2,1)} %bitcast.28), calls=%async_computation.3 | async-start | bytes 524288 | tf_op jit(solution)/shard_map/all_to_all | solution.py:139
  109.8 6.2 %copy-start.8 = (f32[16]{0:T(128)S(1)}, f32[16]{0:T(128)}, u32[]{:S(2)}) copy-start(f32[16]{0:T(128)} %param.20) | copy-start | bytes 196
  109.8 6.3 %copy-start.3 = (s32[1,512,1]{1,2,0:T(1,128)S(1)}, s32[1,512,1]{1,2,0:T(1,128)}, u32[]{:S(2)}) copy-start(s32[1,512,1]{1,2,0:T(1,128)} %param.14) | copy-start | bytes 6148
  109.9 9.0 %copy-start.11 = (f32[16]{0:T(128)S(1)}, f32[16]{0:T(128)}, u32[]{:S(2)}) copy-start(f32[16]{0:T(128)} %param.19) | copy-start | bytes 196
  109.9 9.1 %copy-start.6 = (f32[4,1024]{1,0:T(4,128)S(1)}, f32[4,1024]{1,0:T(4,128)}, u32[]{:S(2)}) copy-start(f32[4,1024]{1,0:T(4,128)} %param.21) | copy-start | bytes 49156
  109.9 10.7 %copy-start.7 = (f32[16]{0:T(128)S(1)}, f32[16]{0:T(128)}, u32[]{:S(2)}) copy-start(f32[16]{0:T(128)} %param.18) | copy-start | bytes 196
  109.9 98.7 %all-to-all-start.2 = ((bf16[8,128,2048]{2,1,0:T(8,128)(2,1)}), bf16[8,128,2048]{2,1,0:T(8,128)(2,1)}, u32[]{:S(2)}, u32[]{:S(2)}) async-start(bf16[8,128,2048]{2,1,0:T(8,128)(2,1)} %bitcast.185), calls=%async_computation.2 | async-start | bytes 8388608 | tf_op jit(solution)/shard_map/all_to_all | solution.py:138
  216.0 1.3 copy-start.2
  217.4 0.7 copy-start.5
  279.7 52.1 %copy-start.9 = (bf16[1,1024,2048]{2,1,0:T(8,128)(2,1)S(1)}, bf16[1,1024,2048]{2,1,0:T(8,128)(2,1)}, u32[]{:S(2)}) copy-start(bf16[1,1024,2048]{2,1,0:T(8,128)(2,1)} %param.23) | copy-start | bytes 12582916
  435.2 53.1 %all-to-all-start.6 = ((bf16[8,4,32,2048]{3,2,0,1:T(8,128)(2,1)}), bf16[8,4,32,2048]{3,2,0,1:T(8,128)(2,1)}, u32[]{:S(2)}, u32[]{:S(2)}) async-start(bf16[8,4,32,2048]{3,2,0,1:T(8,128)(2,1)} %copy.101), calls=%async_computation.6 | async-start | bytes 8388608 | tf_op jit(solution)/shard_map/all_to_all | solution.py:176
  491.4 1.9 copy-start.1
Sparse Core Ops, SparseCore 0:
  42.8 33.4 all-gather.1
where the time goes:
time: 501 us; the launch traced here: 500 us
  blocking collectives  182 us (36%)
  waiting for transfers between devices  160 us (32%)
  matrix products  57.8 us (12%)
  local copies, waits for them, and re-layouts  52.3 us (10%)
  starting transfers between devices  20 us (4%)
  other arithmetic  14.6 us (3%)
  between operations  13.8 us (3%)
    all_to_all x1, blocking collectives, per_device(): lax.all_to_all(parts, 'expert', split_axis=0, concat_axis=0, tiled=True)  96.5 us
    all_to_all x1, waiting for transfers between devices, per_device(): lax.all_to_all(gate_inner, 'expert', split_axis=0, concat_axis=0, tiled=T...  86.1 us
    all_to_all x1, blocking collectives, per_device(): lax.all_to_all(leaving, 'expert', split_axis=0, concat_axis=0, tiled=True)  52.1 us
    all_to_all x1, waiting for transfers between devices, per_device(): lax.all_to_all(lax.all_to_all(parts, 'expert', split_axis=0, concat_axis=...  48.2 us
    all_to_all x1, blocking collectives, per_device(): lax.all_to_all(outgoing, 'expert', split_axis=0, concat_axis=0, tiled=True)  33 us
    all_gather x1, waiting for transfers between devices, per_device(): gathered = lax.all_gather(arrived, 'context', axis=1, tiled=True)  23.2 us
    dot_general x4, matrix products, advance(): local = jnp.einsum('tuh,uhp->thp', weights, values, precision=exact)  16.9 us
    unnamed x28, local copies, waits for them, and re-layouts  16.5 us
  transfers between devices with their start and end apart: 5, of which 4 were waited for; matrix products, arithmetic and copies ran while one was open for 7% of the time, Pallas kernels for 0%

commit v1 on v0

v1 whole, which is shorter than its diff:
```python
import functools

import jax
import jax.numpy as jnp
from jax import lax
from jax.experimental import pallas as pl
from jax.experimental.pallas import tpu as pltpu
from jax.sharding import PartitionSpec as P

HEAD_DIM = 64
LANES = 128
BF16 = jnp.bfloat16
F32 = jnp.float32


def iota(shape, axis):
    return lax.broadcasted_iota(jnp.int32, shape, axis)


def dot(a, b):
    return jnp.dot(a, b, preferred_element_type=F32)


def flat_rows(pieces):
    count, rows, lanes = pieces.shape
    if rows % 16:
        return pieces.astype(F32).reshape(count * rows, lanes).astype(BF16)
    return pieces.reshape(count * rows, lanes)


def slot_rows(ids, experts, cap):
    tok_rows = ids.shape[1]
    onehot = jnp.where(iota((experts, tok_rows), 0) == ids, 1.0, 0.0)
    upto = jnp.where(iota((tok_rows, tok_rows), 0) <= iota((tok_rows, tok_rows), 1), 1.0, 0.0)
    before = dot(onehot.astype(BF16), upto.astype(BF16))
    rank = jnp.sum(onehot * before, axis=0, keepdims=True) - 1.0
    slot = ids * cap + rank.astype(jnp.int32)
    return jnp.where(iota((experts * cap, tok_rows), 0) == slot, 1.0, 0.0)


VMEM = pl.BlockSpec(memory_space=pltpu.VMEM)
SMEM = pl.BlockSpec(memory_space=pltpu.SMEM)
ANY = pl.BlockSpec(memory_space=pl.ANY)


def call(kernel, inputs, outputs, after=(), scratch=(), flops=0, exps=0):
    moved = sum(2 * a.size for a in inputs[1:]) + sum(2 * o.size for o in outputs)
    count = len(inputs)

    def body(*refs):
        kernel(*refs[:count], *refs[count + len(after) :])

    return pl.pallas_call(
        body,
        out_shape=outputs,
        in_specs=[SMEM] + [VMEM] * (count - 1) + [ANY] * len(after),
        out_specs=[VMEM] * len(outputs),
        scratch_shapes=list(scratch),
        compiler_params=pltpu.CompilerParams(vmem_limit_bytes=24 << 20),
        cost_estimate=pl.CostEstimate(flops=flops, bytes_accessed=moved, transcendentals=exps),
    )(*inputs, *after)


def shape(*dims):
    return jax.ShapeDtypeStruct(dims, BF16)


def tie(value, *after):
    return pl.pallas_call(
        lambda *refs: None,
        out_shape=jax.ShapeDtypeStruct(value.shape, value.dtype),
        in_specs=[ANY] * (1 + len(after)),
        out_specs=ANY,
        input_output_aliases={0: 0},
    )(value, *after)


def dispatch_kernel(experts, cap, info_ref, ids_ref, tokens_ref, out_ref):
    place = slot_rows(ids_ref[info_ref[0]], experts, cap).astype(BF16)
    out_ref[...] = dot(place, tokens_ref[...]).astype(BF16)


def collect_kernel(experts, cap, info_ref, ids_ref, rows_ref, out_ref):
    place = slot_rows(ids_ref[info_ref[0]], experts, cap).T.astype(BF16)
    out_ref[...] = dot(place, rows_ref[...]).astype(BF16)


def side_kernel(experts, cap, chans, info_ref, ids_ref, near_ref, out_ref):
    place = slot_rows(ids_ref[info_ref[0]], experts, cap).T.astype(BF16)
    for i in range(2):
        rows = flat_rows(near_ref[:, i, :, chans:])
        out_ref[:, i * LANES : (i + 1) * LANES] = dot(place, rows).astype(BF16)


def sum_kernel(info_ref, *refs):
    total = refs[0][...].astype(F32)
    for ref in refs[1:-1]:
        total = total + ref[...].astype(F32)
    refs[-1][...] = total.astype(BF16)


def project_kernel(places, experts, cap, chans, info_ref, *refs):
    rows, weight, out_ref = refs[:places], refs[places], refs[-1]
    tile = 256
    for lo in range(0, chans, tile):
        for at in range(places):
            made = dot(rows[at][...], weight[:, chans + lo : chans + lo + tile]).astype(BF16)
            for e in range(experts):
                out_ref[e, at, :, lo : lo + tile] = made[e * cap : (e + 1) * cap, :]
    if len(refs) > places + 2:
        made = dot(rows[0][...], refs[places + 1][...]).astype(BF16)
        for at in range(2):
            for e in range(experts):
                out_ref[e, at, :, chans:] = made[
                    e * cap : (e + 1) * cap, at * LANES : (at + 1) * LANES
                ]


def gate_kernel(places, chans, info_ref, *refs):
    rows, weight, outs = refs[:places], refs[places], refs[-places:]
    tile = 256
    for lo in range(0, chans, tile):
        for at in range(places):
            outs[at][:, lo : lo + tile] = dot(rows[at][...], weight[:, lo : lo + tile]).astype(BF16)


def output_kernel(places, first, info_ref, scanned_ref, *refs):
    gates, weight, outs = refs[:places], refs[places], refs[-places:]
    width = weight.shape[1]
    for at in range(places):
        scanned = flat_rows(scanned_ref[:, first + at])
        gate = jax.nn.silu(gates[at][...].astype(F32))
        gated = (scanned.astype(F32) * gate).astype(BF16)
        tile = 512
        for lo in range(0, width, tile):
            outs[at][:, lo : lo + tile] = dot(gated, weight[:, lo : lo + tile]).astype(BF16)


def scan_kernel(
    cfg,
    info_ref,
    ids_ref,
    side_ref,
    head_ref,
    chan_ref,
    near_ref,
    far_ref,
    out_near_ref,
    out_far_ref,
    rows_ref,
    state_ref,
    last_ref,
):
    blocks = ids_ref.shape[0]
    state_ref[...] = jnp.zeros_like(state_ref)
    last_ref[...] = jnp.zeros_like(last_ref)
    block = functools.partial(
        scan_block, cfg, info_ref, ids_ref, side_ref, head_ref, chan_ref, near_ref, far_ref,
        out_near_ref, out_far_ref, rows_ref, state_ref, last_ref,
    )
    pl.loop(0, blocks)(block)


def scan_block(
    cfg,
    info_ref,
    ids_ref,
    side_ref,
    head_ref,
    chan_ref,
    near_ref,
    far_ref,
    out_near_ref,
    out_far_ref,
    rows_ref,
    state_ref,
    last_ref,
    b,
):
    experts, cap, tok_rows, nstate, chn, heads = cfg
    q = info_ref[1 + b]

    def load(ref, at):
        for e in range(experts):
            rows_ref[e * cap : (e + 1) * cap, :] = ref[e, at, :, :chn].astype(rows_ref.dtype)

    @pl.when(q < 2)
    def _():
        load(near_ref, q)

    @pl.when(q >= 2)
    def _():
        load(far_ref, q - 2)

    place_t = slot_rows(ids_ref[b], experts, cap)
    place = place_t.T.astype(BF16)
    place_t = place_t.astype(BF16)

    inner = dot(place, rows_ref[...].astype(BF16))
    both = side_ref[q, :, :LANES]
    own_head = iota((LANES, LANES), 0) == iota((LANES, LANES), 1) + info_ref[1 + ids_ref.shape[0] + b] * heads
    own_head = jnp.where(own_head & (iota((LANES, LANES), 1) < heads), 1.0, 0.0)
    raw = dot(side_ref[q, :, LANES:], own_head.astype(BF16))

    taps = 4
    padded = jnp.concatenate([last_ref[...], inner], axis=0)
    total = chan_ref[taps : taps + 1, :]
    for j in range(taps):
        start = 8 - (taps - 1) + j
        total = total + chan_ref[j : j + 1, :] * padded[start : start + tok_rows, :]
    last_ref[...] = inner[tok_rows - 8 :, :]
    signal = jax.nn.silu(total)

    step = jax.nn.softplus(raw + head_ref[0:1, :])
    logs = step * head_ref[1:2, :]
    lower = iota((tok_rows, tok_rows), 0) >= iota((tok_rows, tok_rows), 1)
    summed = jnp.dot(
        jnp.where(lower, 1.0, 0.0),
        logs,
        preferred_element_type=F32,
        precision=lax.Precision.HIGHEST,
    )
    summed_t = summed.T
    tail = jnp.exp(summed[tok_rows - 1 :, :] - summed) * step

    spread = jnp.where(
        iota((LANES, chn), 0) == iota((LANES, chn), 1) // HEAD_DIM, 1.0, 0.0
    ).astype(BF16)
    spread = jnp.concatenate([spread, spread], axis=0)

    def widen(values):
        high = values.astype(BF16)
        low = (values - high.astype(F32)).astype(BF16)
        return dot(jnp.concatenate([high, low], axis=1), spread)

    step_wide = widen(step)
    kept_wide = widen(jnp.exp(summed))
    tail_wide = widen(tail)

    both_t = both.astype(F32).T.astype(BF16)
    keys_t = both_t[:nstate, :]
    queries = both[:, nstate:]
    scores = dot(queries, keys_t)

    state = state_ref[...]
    carried = dot(queries, state.astype(BF16)) * kept_wide
    rest = carried + chan_ref[taps + 1 : taps + 2, :] * signal
    scaled = (signal * step_wide).astype(BF16)
    state_ref[...] = kept_wide[tok_rows - 1 :, :] * state + dot(
        keys_t, (signal * tail_wide).astype(BF16)
    )

    first = iota((tok_rows, LANES), 1) < HEAD_DIM
    made = []
    for pair in range(heads // 2):
        values = scaled[:, pair * LANES : (pair + 1) * LANES]
        two = []
        for h in (2 * pair, 2 * pair + 1):
            gaps = summed[:, h : h + 1] - summed_t[h : h + 1, :]
            decay = jnp.exp(jnp.where(lower, gaps, -jnp.inf))
            two.append(dot((scores * decay).astype(BF16), values))
        made.append(jnp.where(first, two[0], two[1]))
    scanned = (rest + jnp.concatenate(made, axis=1)).astype(BF16)
    leaving = dot(place_t, scanned).astype(BF16)

    def store(ref, at):
        for e in range(experts):
            ref[e, at] = leaving[e * cap : (e + 1) * cap, :]

    @pl.when(q < 2)
    def _():
        store(out_near_ref, q)

    @pl.when(q >= 2)
    def _():
        store(out_far_ref, q - 2)


def per_device(
    tokens,
    route,
    w_inner,
    w_state,
    w_step,
    step_bias,
    decay_log,
    skip_gain,
    conv_weight,
    conv_bias,
    w_out,
):
    tok_rows, width = tokens.shape[1], tokens.shape[2]
    experts = lax.axis_size("expert")
    shards = lax.axis_size("context")
    cap = 2 * tok_rows // experts
    slots = experts * cap
    chans = w_inner.shape[3]
    heads = w_step.shape[2]
    nstate = w_state.shape[2] // 2
    chips = shards // 2
    far_count = shards - 2

    here = lax.axis_index("context").astype(jnp.int32)
    blocks = jnp.arange(shards, dtype=jnp.int32)
    order = 2 * ((here // 2 - blocks // 2) % chips) + ((here % 2) ^ (blocks % 2))
    groups = 2 * ((blocks // 2 - here // 2) % chips) + ((here % 2) ^ (blocks % 2))
    info = jnp.concatenate([here[None], order, groups])
    ids = route.reshape(shards, 1, tok_rows)
    swap = [(c, c ^ 1) for c in range(shards)]

    def hop(k):
        return [(c, ((c // 2 + k) % chips) * 2 + c % 2) for c in range(shards)]

    def permute(value, pairs):
        return lax.ppermute(value, "context", pairs)

    def spread(value):
        made = [value, permute(value, swap)]
        for k in range(1, chips):
            arrived = permute(value, hop(k))
            made += [arrived, permute(arrived, swap)]
        return made

    def exchange(value):
        return lax.all_to_all(value, "expert", split_axis=0, concat_axis=0, tiled=True)

    w_flat = w_inner[0].reshape(width, 2 * chans)
    steps_t = jnp.concatenate(spread(tie(w_step[0].T, w_flat)))
    all_heads = shards * heads
    w_side = jnp.concatenate(
        [w_state[0], jnp.pad(steps_t, ((0, LANES - all_heads), (0, 0))).T], axis=1
    )

    outgoing = call(
        functools.partial(dispatch_kernel, experts, cap),
        [info, ids, tokens[0]],
        [shape(slots, width)],
        flops=2 * slots * tok_rows * width,
    )[0]
    own = exchange(outgoing.reshape(experts, cap, width)).reshape(slots, width)
    own = tie(own, w_flat, w_side)
    swapped = permute(own, swap)
    near = call(
        functools.partial(project_kernel, 2, experts, cap, chans),
        [info, own, swapped, w_flat, w_side],
        [shape(experts, 2, cap, chans + LANES)],
        flops=4 * slots * width * (chans + LANES),
    )[0]
    distant = []
    for k in range(1, chips):
        arrived = permute(own, hop(k))
        distant += [arrived, permute(tie(arrived, near), swap)]
    far = call(
        functools.partial(project_kernel, far_count, experts, cap, chans),
        [info, *distant, w_flat],
        [shape(experts, far_count, cap, chans)],
        flops=2 * far_count * slots * width * chans,
    )[0]
    near_back = exchange(near)
    far_back = exchange(far)

    side = call(
        functools.partial(side_kernel, experts, cap, chans),
        [info, ids, near_back],
        [shape(tok_rows, 2 * LANES)],
        after=[far],
        flops=2 * slots * tok_rows * 2 * LANES,
    )[0]
    sides = jnp.stack(spread(side))

    def padded_heads(row):
        return jnp.pad(row, (0, LANES - heads))[None, :]

    head_rows = jnp.concatenate(
        [padded_heads(step_bias), padded_heads(-jnp.exp(decay_log)), jnp.zeros((6, LANES), F32)]
    )
    chan_rows = jnp.concatenate(
        [conv_weight, conv_bias[None, :], jnp.repeat(skip_gain, HEAD_DIM)[None, :]]
    )
    chan_rows = jnp.pad(chan_rows, ((0, 2), (0, 0)))
    def gates(rows):
        return call(
            functools.partial(gate_kernel, len(rows), chans),
            [info, *rows, w_flat],
            [shape(slots, chans)] * len(rows),
            after=[far],
            flops=2 * len(rows) * slots * width * chans,
        )

    gate_far = gates(distant)
    gate_near = gates([own, swapped])
    cfg = (experts, cap, tok_rows, nstate, chans, heads)
    near_out, far_out = call(
        functools.partial(scan_kernel, cfg),
        [info, ids, sides, head_rows, chan_rows, near_back, far_back],
        [shape(experts, 2, cap, chans), shape(experts, far_count, cap, chans)],
        after=[gate_far[0], gate_near[0]],
        scratch=[
            pltpu.VMEM((slots, chans), BF16 if cap % 16 == 0 else F32),
            pltpu.VMEM((nstate, chans), F32),
            pltpu.VMEM((8, chans), F32),
        ],
        flops=2 * shards * tok_rows * chans * (2 * slots + 2 * nstate + 2 * tok_rows + 768),
        exps=shards * tok_rows * tok_rows * heads,
    )
    far_ret = exchange(far_out)
    near_ret = exchange(near_out)

    def outputs(scanned, gate, first, after=()):
        return call(
            functools.partial(output_kernel, len(gate), first),
            [info, scanned, *gate, w_out[0]],
            [shape(slots, width)] * len(gate),
            after=after,
            flops=2 * len(gate) * slots * width * chans,
        )

    parts_far = outputs(far_ret, gate_far, 0)
    pairs = []
    for k in range(1, chips):
        mine, other = parts_far[2 * k - 2], parts_far[2 * k - 1]
        pairs.append((mine.astype(F32) + permute(other, swap).astype(F32)).astype(BF16))
    hopped = [permute(pair, hop(chips - k)) for k, pair in enumerate(pairs, 1)]
    part_swap = outputs(near_ret, gate_near[1:], 1)[0]
    part_own = outputs(near_ret, gate_near[:1], 0, hopped)[0]
    summed = call(
        sum_kernel, [info, part_own, permute(part_swap, swap), *hopped], [shape(slots, width)]
    )[0]
    returned = exchange(summed.reshape(experts, cap, width)).reshape(slots, width)
    result = call(
        functools.partial(collect_kernel, experts, cap),
        [info, ids, returned],
        [shape(tok_rows, width)],
        flops=2 * slots * tok_rows * width,
    )[0]
    return result[None]


def solution(mesh):
    in_specs = (
        P("expert", "context", None),
        P("expert", None, None),
        P("expert", None, None, "context"),
        P("expert", None, None),
        P("expert", None, "context"),
        P("context"),
        P("context"),
        P("context"),
        P(None, "context"),
        P("context"),
        P("expert", "context", None),
    )
    out_specs = P("expert", "context", None)
    return jax.shard_map(
        per_device, mesh=mesh, in_specs=in_specs, out_specs=out_specs, check_vma=False
    )
```

time: 501 us -> 235 us (0.47)
  blocking collectives: 182 us -> 60.3 us
  waiting for transfers between devices: 160 us -> 66.8 us
  matrix products: 57.8 us -> 0 us
  Pallas kernels: 0 us -> 36.3 us
  between operations: 13.8 us -> 0.27 us
  local copies, waits for them, and re-layouts: 52.3 us -> 38.8 us
  other arithmetic: 14.6 us -> 3.46 us
  starting transfers between devices: 20 us -> 27.9 us
    all_to_all x3 -> x2, blocking collectives: 182 us -> 60.3 us  [exchange(): lax.all_to_all(value, 'expert', split_axis=0, concat_axis=0, tiled=True)]
    all_to_all x4, waiting for transfers between devices: 137 us -> 33.8 us  [exchange(): lax.all_to_all(value, 'expert', split_axis=0, concat_axis=0, tiled=True)]
    dot_general x21 -> x0, matrix products: 57.8 us -> none  [the longest x4 16.9 us: advance(): local = jnp.einsum('tuh,uhp->thp', weights, values, precision=exact)]
    pallas_call x0 -> x15, Pallas kernels: none -> 36.3 us  [the longest x12 36.3 us: call(): pl.pallas_call(body, out_shape=outputs, in_specs=[SMEM] + [VMEM] * (count...]
    ppermute x0 -> x12, waiting for transfers between devices: none -> 33 us  [permute(): return lax.ppermute(value, 'context', pairs)]
    all_gather x1 -> x0, waiting for transfers between devices: 23.2 us -> none  [per_device(): gathered = lax.all_gather(arrived, 'context', axis=1, tiled=True)]
    unnamed x28 -> x67, local copies, waits for them, and re-layouts: 16.5 us -> 37.4 us
    gather x6 -> x0, local copies, waits for them, and re-layouts: 14.9 us -> none  [the longest x1 7.13 us: per_device(): jnp.take(gate_back.reshape(-1, 2 * chans), seq_slot, axis=0)]
  transfers between devices with their start and end apart: 5 -> 16, of which waited for: 4 -> 10; matrix products, arithmetic and copies ran while one was open for 7% -> 7% of each run, Pallas kernels for 0% -> 9%
where the time goes in v1:
time: 235 us; the launch traced here: 234 us
  waiting for transfers between devices  66.8 us (28%)
  blocking collectives  60.3 us (26%)
  local copies, waits for them, and re-layouts  38.8 us (17%)
  Pallas kernels  36.3 us (15%)
  starting transfers between devices  27.9 us (12%)
  other arithmetic  3.46 us (1%)
    all_to_all x2, blocking collectives, exchange(): lax.all_to_all(value, 'expert', split_axis=0, concat_axis=0, tiled=True)  60.3 us
    unnamed x67, local copies, waits for them, and re-layouts  37.4 us
    pallas_call x12, Pallas kernels, call(): pl.pallas_call(body, out_shape=outputs, in_specs=[SMEM] + [VMEM] * (count...  36.3 us
    all_to_all x4, waiting for transfers between devices, exchange(): lax.all_to_all(value, 'expert', split_axis=0, concat_axis=0, tiled=True)  33.8 us
    ppermute x12, waiting for transfers between devices, permute(): return lax.ppermute(value, 'context', pairs)  33 us
    all_to_all x4, starting transfers between devices, exchange(): lax.all_to_all(value, 'expert', split_axis=0, concat_axis=0, tiled=True)  21.1 us
    ppermute x12, starting transfers between devices, permute(): return lax.ppermute(value, 'context', pairs)  6.88 us
  transfers between devices with their start and end apart: 16, of which 10 were waited for; matrix products, arithmetic and copies ran while one was open for 7% of the time, Pallas kernels for 9%

profile of v1, /device:TPU:0, one launch (start us, length us, event | category | flops | bytes accessed | tf_op | source)
XLA Modules:
  0.0 233.8 jit_solution(6161236184992023933)
XLA Ops:
  5.3 7.3 %all-to-all-start = ((bf16[8,32,2048]{2,1,0:T(8,128)(2,1)}), bf16[8,32,2048]{2,1,0:T(8,128)(2,1)S(1)}, u32[]{:S(2)}, u32[]{:S(2)}) async-start(bf16[8,32,2048]{2,1,0:T(8,128)(2,1)} %bitcast.3), calls=%async_computation | async-start | bytes 2097152 | tf_op jit(solution)/shard_map/all_to_all | solution.py:325
  12.6 10.2 %copy.18 = bf16[256,8,2,1024]{3,1,2,0:T(8,128)(2,1)} copy(bf16[256,8,2,1024]{3,2,1,0:T(2,128)(2,1)} %bitcast.45) | data formatting | bytes 16777216
  25.6 11.9 %collective-permute-done.1 = bf16[16,2048]{0,1:T(8,128)(2,1)S(1)} collective-permute-done((bf16[16,2048]{0,1:T(8,128)(2,1)S(1)}, bf16[16,2048]{0,1:T(8,128)(2,1)S(1)}, u32[]{:S(2)}, u32[]{:S(2)}) %collective-permute-start.1) | collective-permute-done | bytes 65568 | tf_op jit(solution)/shard_map/ppermute | solution.py:315
  45.1 3.4 %copy-done = bf16[256,8,2,1024]{3,1,2,0:T(8,128)(2,1)S(1)} copy-done((bf16[256,8,2,1024]{3,1,2,0:T(8,128)(2,1)S(1)}, bf16[256,8,2,1024]{3,1,2,0:T(8,128)(2,1)}, u32[]{:S(2)}) %copy-start) | copy-done | bytes 8388632
  49.7 4.2 %shard_map.112.refs_1_ = bf16[8,2,32,1152]{3,2,1,0:T(8,128)(2,1)} custom-call(s32[9]{0:T(128)S(1)} %pad_add_fusion.refs_0_, bf16[256,2048]{1,0:T(8,128)(2,1)S(1)} %copy-done.6, bf16[256,2048]{1,0:T(8,128)(2,1)S(1)} %collective-permute-done.3.refs_2_, bf16[2048,2048]{1,0:T(8,128)(2,1)S(1)} %bitcast.29, bf16[2048,256]{1,0:T(8,128)(2,1)S(1)} %copy-done.8), custom_call_target="tpu_custom_call" | custom-call | flops 2415919104 | bytes 12713984 | tf_op jit(solution)/shard_map/pallas_call | solution.py:53
  54.9 5.7 %all-to-all-start.1 = ((bf16[8,2,32,1152]{3,2,1,0:T(8,128)(2,1)}), bf16[8,2,32,1152]{3,2,1,0:T(8,128)(2,1)S(1)}, u32[]{:S(2)}, u32[]{:S(2)}) async-start(bf16[8,2,32,1152]{3,2,1,0:T(8,128)(2,1)} %shard_map.112.refs_1_), calls=%async_computation.1 | async-start | bytes 2359296 | tf_op jit(solution)/shard_map/all_to_all | solution.py:325
  60.6 7.4 %collective-permute-done.4.refs_1_ = bf16[256,2048]{1,0:T(8,128)(2,1)S(1)} collective-permute-done((bf16[256,2048]{1,0:T(8,128)(2,1)}, bf16[256,2048]{1,0:T(8,128)(2,1)S(1)}, u32[]{:S(2)}, u32[]{:S(2)}) %collective-permute-start.4) | collective-permute-done | bytes 1048608 | tf_op jit(solution)/shard_map/ppermute | solution.py:315
  69.0 2.9 %collective-permute-done.5.refs_2_ = bf16[256,2048]{1,0:T(8,128)(2,1)S(1)} collective-permute-done((bf16[256,2048]{1,0:T(8,128)(2,1)}, bf16[256,2048]{1,0:T(8,128)(2,1)S(1)}, u32[]{:S(2)}, u32[]{:S(2)}) %collective-permute-start.5) | collective-permute-done | bytes 1048608 | tf_op jit(solution)/shard_map/ppermute | solution.py:315
  71.9 3.4 %copy-done.1 = bf16[256,8,2,1024]{3,1,2,0:T(8,128)(2,1)S(1)} copy-done((bf16[256,8,2,1024]{3,1,2,0:T(8,128)(2,1)S(1)}, bf16[256,8,2,1024]{3,1,2,0:T(8,128)(2,1)}, u32[]{:S(2)}) %copy-start.1) | copy-done | bytes 8388632
  75.3 3.9 %shard_map.114.refs_3_.refs_4_ = bf16[8,2,32,1024]{3,2,1,0:T(8,128)(2,1)} custom-call(s32[9]{0:T(128)S(1)} %pad_add_fusion.refs_0_, bf16[256,2048]{1,0:T(8,128)(2,1)S(1)} %collective-permute-done.4.refs_1_, bf16[256,2048]{1,0:T(8,128)(2,1)S(1)} %collective-permute-done.5.refs_2_, bf16[2048,2048]{1,0:T(8,128)(2,1)S(1)} %bitcast.30), custom_call_target="tpu_custom_call" | custom-call | flops 2147483648 | bytes 11534336 | tf_op jit(solution)/shard_map/pallas_call | solution.py:53
  80.2 9.3 %all-to-all-done.1.refs_2_.refs_5_ = bf16[8,2,32,1152]{3,2,1,0:T(8,128)(2,1)S(1)} async-done(((bf16[8,2,32,1152]{3,2,1,0:T(8,128)(2,1)}), bf16[8,2,32,1152]{3,2,1,0:T(8,128)(2,1)S(1)}, u32[]{:S(2)}, u32[]{:S(2)}) %all-to-all-start.1) | async-done | bytes 1179680 | tf_op jit(solution)/shard_map/all_to_all | solution.py:325
  89.5 4.4 %all-to-all-start.2 = ((bf16[8,2,32,1024]{3,2,1,0:T(8,128)(2,1)}), bf16[8,2,32,1024]{3,2,1,0:T(8,128)(2,1)}, u32[]{:S(2)}, u32[]{:S(2)}) async-start(bf16[8,2,32,1024]{3,2,1,0:T(8,128)(2,1)} %shard_map.114.refs_3_.refs_4_), calls=%async_computation.2 | async-start | bytes 2097152 | tf_op jit(solution)/shard_map/all_to_all | solution.py:325
  96.8 3.4 %copy-done.2 = bf16[256,8,2,1024]{3,1,2,0:T(8,128)(2,1)S(1)} copy-done((bf16[256,8,2,1024]{3,1,2,0:T(8,128)(2,1)S(1)}, bf16[256,8,2,1024]{3,1,2,0:T(8,128)(2,1)}, u32[]{:S(2)}) %copy-start.2) | copy-done | bytes 8388632
  100.2 2.9 %shard_map.117 = (bf16[256,1024]{1,0:T(8,128)(2,1)S(1)}, bf16[256,1024]{1,0:T(8,128)(2,1)S(1)}) custom-call(s32[9]{0:T(128)S(1)} %pad_add_fusion.refs_0_, bf16[256,2048]{1,0:T(8,128)(2,1)S(1)} %copy-done.7, bf16[256,2048]{1,0:T(8,128)(2,1)S(1)} %copy-done.10, bf16[2048,2048]{1,0:T(8,128)(2,1)S(1)} %bitcast.31, ...), custom_call_target="tpu_custom_call" | custom-call | flops 2147483648 | bytes 11534336 | tf_op jit(solution)/shard_map/pallas_call | solution.py:53
  105.2 2.9 %shard_map.116 = (bf16[256,1024]{1,0:T(8,128)(2,1)S(1)}, bf16[256,1024]{1,0:T(8,128)(2,1)S(1)}) custom-call(s32[9]{0:T(128)S(1)} %pad_add_fusion.refs_0_, bf16[256,2048]{1,0:T(8,128)(2,1)S(1)} %collective-permute-done.4.refs_1_, bf16[256,2048]{1,0:T(8,128)(2,1)S(1)} %copy-done.12, bf16[2048,2048]{1,0:T(8,128)(2,1)S(1)} %bitcast.32, ...), custom_call_target="tpu_custom_call" | custom-call | flops 2147483648 | bytes 11534336 | tf_op jit(solution)/shard_map/pallas_call | solution.py:53
  109.7 9.7 %all-to-all-done.2.refs_6_ = bf16[8,2,32,1024]{3,2,1,0:T(8,128)(2,1)} async-done(((bf16[8,2,32,1024]{3,2,1,0:T(8,128)(2,1)}), bf16[8,2,32,1024]{3,2,1,0:T(8,128)(2,1)}, u32[]{:S(2)}, u32[]{:S(2)}) %all-to-all-start.2) | async-done | bytes 1048608 | tf_op jit(solution)/shard_map/all_to_all | solution.py:325
  120.4 10.1 %shard_map.118 = (bf16[8,2,32,1024]{3,2,1,0:T(8,128)(2,1)}, bf16[8,2,32,1024]{3,2,1,0:T(8,128)(2,1)S(1)}) custom-call(s32[9]{0:T(128)S(1)} %pad_add_fusion.refs_0_, s32[4,1,128]{2,1,0:T(1,128)S(1)} %bitcast.43, bf16[4,128,256]{2,1,0:T(8,128)(2,1)S(1)} %pad_maximum_fusion.1.refs_2_, f32[8,128]{1,0:T(8,128)S(1)} %maximum_maximum_fusion.refs_3_, ...), custom_call_target="tpu_custom_call" | custom-call | flops 1744830464 | bytes 4606976 | tf_op jit(solution)/shard_map/pallas_call | solution.py:53
  130.6 29.2 %all_to_all.30.refs_1_ = bf16[8,2,32,1024]{3,2,1,0:T(8,128)(2,1)S(1)} all-to-all(bf16[8,2,32,1024]{3,2,1,0:T(8,128)(2,1)S(1)} %get-tuple-element.16), channel_id=1, replica_groups=mesh['expert'=8,'context'=4] {'expert'}, dimensions={0} | all-to-all | bytes 2097152 | tf_op jit(solution)/shard_map/all_to_all | solution.py:325
  159.7 3.6 %all-to-all-start.3 = ((bf16[8,2,32,1024]{3,2,1,0:T(8,128)(2,1)}), bf16[8,2,32,1024]{3,2,1,0:T(8,128)(2,1)S(1)}, u32[]{:S(2)}, u32[]{:S(2)}) async-start(bf16[8,2,32,1024]{3,2,1,0:T(8,128)(2,1)} %get-tuple-element.15), calls=%async_computation.3 | async-start | bytes 2097152 | tf_op jit(solution)/shard_map/all_to_all | solution.py:325
  165.6 3.0 %shard_map.119 = (bf16[256,2048]{1,0:T(8,128)(2,1)S(1)}, bf16[256,2048]{1,0:T(8,128)(2,1)S(1)}) custom-call(s32[9]{0:T(128)S(1)} %pad_add_fusion.refs_0_, bf16[8,2,32,1024]{3,2,1,0:T(8,128)(2,1)S(1)} %all_to_all.30.refs_1_, bf16[256,1024]{1,0:T(8,128)(2,1)S(1)} %copy-done.23, bf16[256,1024]{1,0:T(8,128)(2,1)S(1)} %copy-done.25, bf16[1024,2048]{1,0:T(8,128)(2,1)S(1)} %bitcast.33), custom_call_target="tpu_custom_call" | custom-call | flops 2147483648 | bytes 8388608 | tf_op jit(solution)/shard_map/pallas_call | solution.py:53
  168.6 2.6 %collective-permute-done.9 = bf16[256,2048]{1,0:T(8,128)(2,1)S(1)} collective-permute-done((bf16[256,2048]{1,0:T(8,128)(2,1)S(1)}, bf16[256,2048]{1,0:T(8,128)(2,1)S(1)}, u32[]{:S(2)}, u32[]{:S(2)}) %collective-permute-start.9) | collective-permute-done | bytes 1048608 | tf_op jit(solution)/shard_map/ppermute | solution.py:315
  174.1 14.8 %all-to-all-done.3.refs_1_ = bf16[8,2,32,1024]{3,2,1,0:T(8,128)(2,1)S(1)} async-done(((bf16[8,2,32,1024]{3,2,1,0:T(8,128)(2,1)}), bf16[8,2,32,1024]{3,2,1,0:T(8,128)(2,1)S(1)}, u32[]{:S(2)}, u32[]{:S(2)}) %all-to-all-start.3) | async-done | bytes 1048608 | tf_op jit(solution)/shard_map/all_to_all | solution.py:325
  193.1 5.0 %collective-permute-done.10.refs_4_.refs_3_ = bf16[256,2048]{1,0:T(8,128)(2,1)S(1)} collective-permute-done((bf16[256,2048]{1,0:T(8,128)(2,1)}, bf16[256,2048]{1,0:T(8,128)(2,1)S(1)}, u32[]{:S(2)}, u32[]{:S(2)}) %collective-permute-start.10) | collective-permute-done | bytes 1048608 | tf_op jit(solution)/shard_map/ppermute | solution.py:315
  200.9 31.1 %all_to_all.31 = bf16[8,32,2048]{2,1,0:T(8,128)(2,1)S(1)} all-to-all(bf16[8,32,2048]{2,1,0:T(8,128)(2,1)S(1)} %bitcast.37), channel_id=1, replica_groups=mesh['expert'=8,'context'=4] {'expert'}, dimensions={0} | all-to-all | bytes 2097152 | tf_op jit(solution)/shard_map/all_to_all | solution.py:325
  (107 shorter events, 41.3 us)
Async XLA Ops:
  5.3 35.9 %all-to-all-start = ((bf16[8,32,2048]{2,1,0:T(8,128)(2,1)}), bf16[8,32,2048]{2,1,0:T(8,128)(2,1)S(1)}, u32[]{:S(2)}, u32[]{:S(2)}) async-start(bf16[8,32,2048]{2,1,0:T(8,128)(2,1)} %bitcast.3), calls=%async_computation | async-start | bytes 2097152 | tf_op jit(solution)/shard_map/all_to_all | solution.py:325
  22.8 17.3 %copy-start.26 = (bf16[1,2048,128]{2,1,0:T(8,128)(2,1)S(1)}, bf16[1,2048,128]{2,1,0:T(8,128)(2,1)}, u32[]{:S(2)}) copy-start(bf16[1,2048,128]{2,1,0:T(8,128)(2,1)} %param.14) | copy-start | bytes 1572868
  24.0 13.5 %collective-permute-start.1 = (bf16[16,2048]{0,1:T(8,128)(2,1)S(1)}, bf16[16,2048]{0,1:T(8,128)(2,1)S(1)}, u32[]{:S(2)}, u32[]{:S(2)}) collective-permute-start(bf16[16,2048]{0,1:T(8,128)(2,1)S(1)} %copy.17), channel_id=1, source_target_pairs={{0,2},{1,3},{2,0},{3,1},{4,6},{5,7},{6,4},{7,5},{8,10},{9,11},{10,... | collective-permute-start | bytes 196616 | tf_op jit(solution)/shard_map/ppermute | solution.py:315
  25.6 11.9 %collective-permute-start = (bf16[16,2048]{0,1:T(8,128)(2,1)S(1)}, bf16[16,2048]{0,1:T(8,128)(2,1)S(1)}, u32[]{:S(2)}, u32[]{:S(2)}) collective-permute-start(bf16[16,2048]{0,1:T(8,128)(2,1)S(1)} %copy.17), channel_id=1, source_target_pairs={{0,1},{1,0},{2,3},{3,2},{4,5},{5,4},{6,7},{7,6},{8,9},{9,8},{10,11... | collective-permute-start | bytes 196616 | tf_op jit(solution)/shard_map/ppermute | solution.py:315
  37.5 1.9 collective-permute-start.2
  42.2 2.9 %collective-permute-start.3 = (bf16[256,2048]{1,0:T(8,128)(2,1)}, bf16[256,2048]{1,0:T(8,128)(2,1)S(1)}, u32[]{:S(2)}, u32[]{:S(2)}) collective-permute-start(bf16[256,2048]{1,0:T(8,128)(2,1)} %shard_map.111.refs_1_), channel_id=1, source_target_pairs={{0,1},{1,0},{2,3},{3,2},{4,5},{5,4},{6,7},{7,6},{8,9},{9,8},{10,11... | collective-permute-start | bytes 3145736 | tf_op jit(solution)/shard_map/ppermute | solution.py:315
  42.4 25.6 %collective-permute-start.4 = (bf16[256,2048]{1,0:T(8,128)(2,1)}, bf16[256,2048]{1,0:T(8,128)(2,1)S(1)}, u32[]{:S(2)}, u32[]{:S(2)}) collective-permute-start(bf16[256,2048]{1,0:T(8,128)(2,1)} %shard_map.111.refs_1_), channel_id=1, source_target_pairs={{0,2},{1,3},{2,0},{3,1},{4,6},{5,7},{6,4},{7,5},{8,10},{9,11},{10,... | collective-permute-start | bytes 3145736 | tf_op jit(solution)/shard_map/ppermute | solution.py:315
  54.9 34.6 %all-to-all-start.1 = ((bf16[8,2,32,1152]{3,2,1,0:T(8,128)(2,1)}), bf16[8,2,32,1152]{3,2,1,0:T(8,128)(2,1)S(1)}, u32[]{:S(2)}, u32[]{:S(2)}) async-start(bf16[8,2,32,1152]{3,2,1,0:T(8,128)(2,1)} %shard_map.112.refs_1_), calls=%async_computation.1 | async-start | bytes 2359296 | tf_op jit(solution)/shard_map/all_to_all | solution.py:325
  69.0 2.9 %collective-permute-start.5 = (bf16[256,2048]{1,0:T(8,128)(2,1)}, bf16[256,2048]{1,0:T(8,128)(2,1)S(1)}, u32[]{:S(2)}, u32[]{:S(2)}) collective-permute-start(bf16[256,2048]{1,0:T(8,128)(2,1)} %shard_map.113), channel_id=1, source_target_pairs={{0,1},{1,0},{2,3},{3,2},{4,5},{5,4},{6,7},{7,6},{8,9},{9,8},{10,11... | collective-permute-start | bytes 3145736 | tf_op jit(solution)/shard_map/ppermute | solution.py:315
  80.2 14.0 %copy-start.28 = (f32[1024]{0:T(1024)S(1)}, f32[1024]{0:T(1024)}, u32[]{:S(2)}) copy-start(f32[1024]{0:T(1024)} %param.20) | copy-start | bytes 12292
  80.2 14.1 %copy-start.20 = (s32[1,512,1]{1,2,0:T(1,128)S(1)}, s32[1,512,1]{1,2,0:T(1,128)}, u32[]{:S(2)}) copy-start(s32[1,512,1]{1,2,0:T(1,128)} %param.12) | copy-start | bytes 6148
  80.2 16.6 %copy-start.7 = (bf16[256,2048]{1,0:T(8,128)(2,1)S(1)}, bf16[256,2048]{1,0:T(8,128)(2,1)}, u32[]{:S(2)}) copy-start(bf16[256,2048]{1,0:T(8,128)(2,1)} %shard_map.111.refs_1_) | copy-start | bytes 3145732
  89.5 29.9 %all-to-all-start.2 = ((bf16[8,2,32,1024]{3,2,1,0:T(8,128)(2,1)}), bf16[8,2,32,1024]{3,2,1,0:T(8,128)(2,1)}, u32[]{:S(2)}, u32[]{:S(2)}) async-start(bf16[8,2,32,1024]{3,2,1,0:T(8,128)(2,1)} %shard_map.114.refs_3_.refs_4_), calls=%async_computation.2 | async-start | bytes 2097152 | tf_op jit(solution)/shard_map/all_to_all | solution.py:325
  95.2 9.4 %collective-permute-start.7 = (bf16[128,256]{1,0:T(8,128)(2,1)S(1)}, bf16[128,256]{1,0:T(8,128)(2,1)S(1)}, u32[]{:S(2)}, u32[]{:S(2)}) collective-permute-start(bf16[128,256]{1,0:T(8,128)(2,1)S(1)} %shard_map.115), channel_id=1, source_target_pairs={{0,2},{1,3},{2,0},{3,1},{4,6},{5,7},{6,4},{7,5},{8,10},{9,11},{10,... | collective-permute-start | bytes 196616 | tf_op jit(solution)/shard_map/ppermute | solution.py:315
  104.6 5.0 %collective-permute-start.6 = (bf16[128,256]{1,0:T(8,128)(2,1)S(1)}, bf16[128,256]{1,0:T(8,128)(2,1)S(1)}, u32[]{:S(2)}, u32[]{:S(2)}) collective-permute-start(bf16[128,256]{1,0:T(8,128)(2,1)S(1)} %shard_map.115), channel_id=1, source_target_pairs={{0,1},{1,0},{2,3},{3,2},{4,5},{5,4},{6,7},{7,6},{8,9},{9,8},{10,11... | collective-permute-start | bytes 196616 | tf_op jit(solution)/shard_map/ppermute | solution.py:315
  104.6 14.7 %copy-start.15 = (bf16[256,1024]{1,0:T(8,128)(2,1)S(1)}, bf16[256,1024]{1,0:T(8,128)(2,1)}, u32[]{:S(2)}) copy-start(bf16[256,1024]{1,0:T(8,128)(2,1)} %copy-done.14) | copy-start | bytes 1572868
  104.7 5.0 %collective-permute-start.8 = (bf16[128,256]{1,0:T(8,128)(2,1)S(1)}, bf16[128,256]{1,0:T(8,128)(2,1)S(1)}, u32[]{:S(2)}, u32[]{:S(2)}) collective-permute-start(bf16[128,256]{1,0:T(8,128)(2,1)S(1)} %collective-permute-done.7), channel_id=1, source_target_pairs={{0,1},{1,0},{2,3},{3,2},{4,5},{5,4},{6,7},{7,6},{8,9},{9,8},{10,11... | collective-permute-start | bytes 196616 | tf_op jit(solution)/shard_map/ppermute | solution.py:315
  130.5 32.8 %copy-start.23 = (bf16[256,1024]{1,0:T(8,128)(2,1)S(1)}, bf16[256,1024]{1,0:T(8,128)(2,1)}, u32[]{:S(2)}) copy-start(bf16[256,1024]{1,0:T(8,128)(2,1)} %copy-done.21) | copy-start | bytes 1572868
  130.6 32.8 %copy-start.25 = (bf16[256,1024]{1,0:T(8,128)(2,1)S(1)}, bf16[256,1024]{1,0:T(8,128)(2,1)}, u32[]{:S(2)}) copy-start(bf16[256,1024]{1,0:T(8,128)(2,1)} %copy-done.24) | copy-start | bytes 1572868
  159.7 29.2 %all-to-all-start.3 = ((bf16[8,2,32,1024]{3,2,1,0:T(8,128)(2,1)}), bf16[8,2,32,1024]{3,2,1,0:T(8,128)(2,1)S(1)}, u32[]{:S(2)}, u32[]{:S(2)}) async-start(bf16[8,2,32,1024]{3,2,1,0:T(8,128)(2,1)} %get-tuple-element.15), calls=%async_computation.3 | async-start | bytes 2097152 | tf_op jit(solution)/shard_map/all_to_all | solution.py:325
  168.6 20.4 %copy-start.18 = (bf16[256,1024]{1,0:T(8,128)(2,1)S(1)}, bf16[256,1024]{1,0:T(8,128)(2,1)}, u32[]{:S(2)}) copy-start(bf16[256,1024]{1,0:T(8,128)(2,1)} %copy-done.17) | copy-start | bytes 1572868
  168.6 2.7 %collective-permute-start.9 = (bf16[256,2048]{1,0:T(8,128)(2,1)S(1)}, bf16[256,2048]{1,0:T(8,128)(2,1)S(1)}, u32[]{:S(2)}, u32[]{:S(2)}) collective-permute-start(bf16[256,2048]{1,0:T(8,128)(2,1)S(1)} %get-tuple-element.19), channel_id=1, source_target_pairs={{0,1},{1,0},{2,3},{3,2},{4,5},{5,4},{6,7},{7,6},{8,9},{9,8},{10,11... | collective-permute-start | bytes 3145736 | tf_op jit(solution)/shard_map/ppermute | solution.py:315
  172.7 25.4 %collective-permute-start.10 = (bf16[256,2048]{1,0:T(8,128)(2,1)}, bf16[256,2048]{1,0:T(8,128)(2,1)S(1)}, u32[]{:S(2)}, u32[]{:S(2)}) collective-permute-start(bf16[256,2048]{1,0:T(8,128)(2,1)} %add_convert_fusion), channel_id=1, source_target_pairs={{0,2},{1,3},{2,0},{3,1},{4,6},{5,7},{6,4},{7,5},{8,10},{9,11},{10,... | collective-permute-start | bytes 3145736 | tf_op jit(solution)/shard_map/ppermute | solution.py:315
  193.0 6.9 %collective-permute-start.11 = (bf16[256,2048]{1,0:T(8,128)(2,1)S(1)}, bf16[256,2048]{1,0:T(8,128)(2,1)S(1)}, u32[]{:S(2)}, u32[]{:S(2)}) collective-permute-start(bf16[256,2048]{1,0:T(8,128)(2,1)S(1)} %shard_map.121), channel_id=1, source_target_pairs={{0,1},{1,0},{2,3},{3,2},{4,5},{5,4},{6,7},{7,6},{8,9},{9,8},{10,11... | collective-permute-start | bytes 3145736 | tf_op jit(solution)/shard_map/ppermute | solution.py:315
  (24 other events, 97.9 us)

commit v2 on v1

v2 whole, which is shorter than its diff:
```python
import functools

import jax
import jax.numpy as jnp
from jax import lax
from jax.experimental import pallas as pl
from jax.experimental.pallas import tpu as pltpu
from jax.sharding import PartitionSpec as P

HEAD_DIM = 64
LANES = 128
BF16 = jnp.bfloat16
F32 = jnp.float32


def iota(shape, axis):
    return lax.broadcasted_iota(jnp.int32, shape, axis)


def dot(a, b):
    return jnp.dot(a, b, preferred_element_type=F32)


def flat_rows(pieces):
    count, rows, lanes = pieces.shape
    if rows % 16:
        return pieces.astype(F32).reshape(count * rows, lanes).astype(BF16)
    return pieces.reshape(count * rows, lanes)


def slot_rows(ids, experts, cap):
    tok_rows = ids.shape[1]
    onehot = jnp.where(iota((experts, tok_rows), 0) == ids, 1.0, 0.0)
    upto = jnp.where(iota((tok_rows, tok_rows), 0) <= iota((tok_rows, tok_rows), 1), 1.0, 0.0)
    before = dot(onehot.astype(BF16), upto.astype(BF16))
    rank = jnp.sum(onehot * before, axis=0, keepdims=True) - 1.0
    slot = ids * cap + rank.astype(jnp.int32)
    return jnp.where(iota((experts * cap, tok_rows), 0) == slot, 1.0, 0.0)


VMEM = pl.BlockSpec(memory_space=pltpu.VMEM)
SMEM = pl.BlockSpec(memory_space=pltpu.SMEM)
ANY = pl.BlockSpec(memory_space=pl.ANY)


def call(kernel, inputs, outputs, streamed=(), after=(), scratch=(), flops=0, exps=0):
    moved = sum(2 * a.size for a in (*streamed, *inputs[1:])) + sum(2 * o.size for o in outputs)
    count = len(streamed) + len(inputs)

    def body(*refs):
        kernel(*refs[:count], *refs[count + len(after) :])

    return pl.pallas_call(
        body,
        out_shape=outputs,
        in_specs=[ANY] * len(streamed) + [SMEM] + [VMEM] * (len(inputs) - 1) + [ANY] * len(after),
        out_specs=[VMEM] * len(outputs),
        scratch_shapes=list(scratch),
        compiler_params=pltpu.CompilerParams(vmem_limit_bytes=24 << 20),
        cost_estimate=pl.CostEstimate(flops=flops, bytes_accessed=moved, transcendentals=exps),
    )(*streamed, *inputs, *after)


def tiles_of(source, held, sems, first, tile):
    count = held.shape[1] // tile
    copies = [
        pltpu.make_async_copy(
            source.at[:, pl.ds(first + t * tile, tile)], held.at[:, pl.ds(t * tile, tile)], sems.at[t]
        )
        for t in range(count)
    ]
    for copy in copies:
        copy.start()

    def tile_at(t):
        copies[t].wait()
        return held[:, t * tile : (t + 1) * tile]

    return tile_at


def held_weight(rows, columns, tile):
    return [pltpu.VMEM((rows, columns), BF16), pltpu.SemaphoreType.DMA((columns // tile,))]


def shape(*dims):
    return jax.ShapeDtypeStruct(dims, BF16)


def tie(value, *after):
    return pl.pallas_call(
        lambda *refs: None,
        out_shape=jax.ShapeDtypeStruct(value.shape, value.dtype),
        in_specs=[ANY] * (1 + len(after)),
        out_specs=ANY,
        input_output_aliases={0: 0},
    )(value, *after)


def dispatch_kernel(experts, cap, info_ref, ids_ref, tokens_ref, out_ref):
    place = slot_rows(ids_ref[info_ref[0]], experts, cap).astype(BF16)
    out_ref[...] = dot(place, tokens_ref[...]).astype(BF16)


def collect_kernel(experts, cap, info_ref, ids_ref, rows_ref, out_ref):
    place = slot_rows(ids_ref[info_ref[0]], experts, cap).T.astype(BF16)
    out_ref[...] = dot(place, rows_ref[...]).astype(BF16)


def side_kernel(experts, cap, chans, info_ref, ids_ref, near_ref, out_ref):
    place = slot_rows(ids_ref[info_ref[0]], experts, cap).T.astype(BF16)
    for i in range(2):
        rows = flat_rows(near_ref[:, i, :, chans:])
        out_ref[:, i * LANES : (i + 1) * LANES] = dot(place, rows).astype(BF16)


def sum_kernel(info_ref, *refs):
    total = refs[0][...].astype(F32)
    for ref in refs[1:-1]:
        total = total + ref[...].astype(F32)
    refs[-1][...] = total.astype(BF16)


def project_kernel(places, experts, cap, chans, weight_ref, info_ref, *refs):
    rows, sides, (out_ref, held, sems) = refs[:places], refs[places:-3], refs[-3:]
    tile = 256
    tile_at = tiles_of(weight_ref, held, sems, chans, tile)

    def store(at, lo, made):
        made = made.astype(BF16)
        for e in range(experts):
            out_ref[e, at, :, lo : lo + made.shape[1]] = made[e * cap : (e + 1) * cap, :]

    if sides:
        store(0, chans, dot(rows[0][...], sides[0][...]))
        steps = [ref[...].astype(F32) for ref in sides[1:]]
        spare = LANES - sum(part.shape[0] for part in steps)
        steps.append(jnp.zeros((spare, steps[0].shape[1]), F32))
        steps = jnp.concatenate(steps, axis=0).astype(BF16)
        made = lax.dot_general(
            rows[0][...], steps, (((1,), (1,)), ((), ())), preferred_element_type=F32
        )
        store(1, chans, made)
    for t in range(chans // tile):
        weight = tile_at(t)
        for at in range(places):
            store(at, t * tile, dot(rows[at][...], weight))


def gate_kernel(places, chans, weight_ref, info_ref, *refs):
    rows, outs, (held, sems) = refs[:places], refs[places:-2], refs[-2:]
    tile = 256
    tile_at = tiles_of(weight_ref, held, sems, 0, tile)
    for t in range(chans // tile):
        weight = tile_at(t)
        for at in range(places):
            outs[at][:, t * tile : (t + 1) * tile] = dot(rows[at][...], weight).astype(BF16)


def output_kernel(places, weight_ref, info_ref, scanned_ref, *refs):
    count = len(places)
    gates, outs, (held, sems) = refs[:count], refs[count:-2], refs[-2:]
    tile = 512
    tile_at = tiles_of(weight_ref, held, sems, 0, tile)
    gated = []
    for gate_ref, at in zip(gates, places):
        scanned = flat_rows(scanned_ref[:, at]).astype(F32)
        gated.append((scanned * jax.nn.silu(gate_ref[...].astype(F32))).astype(BF16))
    for t in range(held.shape[1] // tile):
        weight = tile_at(t)
        for rows, out in zip(gated, outs):
            out[:, t * tile : (t + 1) * tile] = dot(rows, weight).astype(BF16)


def scan_kernel(
    cfg,
    info_ref,
    ids_ref,
    side_ref,
    head_ref,
    chan_ref,
    near_ref,
    far_ref,
    out_near_ref,
    out_far_ref,
    inner_ref,
    made_ref,
):
    experts, cap, tok_rows, nstate, chn, heads = cfg
    blocks = ids_ref.shape[0]
    taps = 4
    inner_ref[:8, :] = jnp.zeros((8, chn), F32)

    for q in range(blocks):
        b = info_ref[1 + q]
        place = slot_rows(ids_ref[b], experts, cap).T.astype(BF16)
        rows = flat_rows(near_ref[:, q, :, :chn] if q < 2 else far_ref[:, q - 2])
        inner_ref[pl.ds(8 + b * tok_rows, tok_rows), :] = dot(place, rows)

    lower = iota((tok_rows, tok_rows), 0) >= iota((tok_rows, tok_rows), 1)
    ones = jnp.where(lower, 1.0, 0.0)
    first = iota((tok_rows, LANES), 1) < HEAD_DIM
    spread = jnp.where(
        iota((2 * LANES, chn), 0) % LANES == iota((2 * LANES, chn), 1) // HEAD_DIM, 1.0, 0.0
    ).astype(BF16)

    def widen(values):
        high = values.astype(BF16)
        low = (values - high.astype(F32)).astype(BF16)
        return dot(jnp.concatenate([high, low], axis=1), spread)

    state = jnp.zeros((nstate, chn), F32)
    for b in range(blocks):
        q = info_ref[1 + blocks + b]
        total = chan_ref[taps : taps + 1, :]
        for j in range(taps):
            start = 8 + b * tok_rows - (taps - 1) + j
            total = total + chan_ref[j : j + 1, :] * inner_ref[start : start + tok_rows, :]
        signal = jax.nn.silu(total)

        own_head = iota((LANES, LANES), 0) == iota((LANES, LANES), 1) + info_ref[
            1 + 2 * blocks + b
        ] * heads
        own_head = jnp.where(own_head & (iota((LANES, LANES), 1) < heads), 1.0, 0.0)
        raw = dot(side_ref[q, :, LANES:], own_head.astype(BF16))
        step = jax.nn.softplus(raw + head_ref[0:1, :])
        summed = jnp.dot(
            ones,
            step * head_ref[1:2, :],
            preferred_element_type=F32,
            precision=lax.Precision.HIGHEST,
        )
        source = summed - jnp.log(step)
        source_t = source.T
        kept = widen(jnp.exp(summed))
        tail = widen(jnp.exp(summed[tok_rows - 1 :, :] - source))

        both = side_ref[q, :, :LANES]
        keys_t = both.astype(F32).T.astype(BF16)[:nstate, :]
        queries = both[:, nstate:]
        scores = dot(queries, keys_t)
        rest = chan_ref[taps + 1 : taps + 2, :] * signal
        if b > 0:
            rest = rest + dot(queries, state.astype(BF16)) * kept
        if b < blocks - 1:
            state = kept[tok_rows - 1 :, :] * state + dot(keys_t, (signal * tail).astype(BF16))

        for pair in range(heads // 2):
            lanes = slice(pair * LANES, (pair + 1) * LANES)
            values = signal[:, lanes]
            values = jnp.concatenate(
                [jnp.where(first, values, 0.0), jnp.where(first, 0.0, values)], axis=0
            ).astype(BF16)
            weights = []
            for h in (2 * pair, 2 * pair + 1):
                gaps = summed[:, h : h + 1] - source_t[h : h + 1, :]
                decay = jnp.exp(jnp.where(lower, gaps, -jnp.inf))
                weights.append((scores * decay).astype(BF16))
            local = dot(jnp.concatenate(weights, axis=1), values)
            made_ref[b * tok_rows : (b + 1) * tok_rows, lanes] = (rest[:, lanes] + local).astype(BF16)

    for q in range(blocks):
        b = info_ref[1 + q]
        place = slot_rows(ids_ref[b], experts, cap).astype(BF16)
        start = pl.multiple_of(b * tok_rows, tok_rows)
        leaving = dot(place, made_ref[pl.ds(start, tok_rows), :]).astype(BF16)
        for e in range(experts):
            piece = leaving[e * cap : (e + 1) * cap, :]
            if q < 2:
                out_near_ref[e, q] = piece
            else:
                out_far_ref[e, q - 2] = piece


def per_device(
    tokens,
    route,
    w_inner,
    w_state,
    w_step,
    step_bias,
    decay_log,
    skip_gain,
    conv_weight,
    conv_bias,
    w_out,
):
    tok_rows, width = tokens.shape[1], tokens.shape[2]
    experts = lax.axis_size("expert")
    shards = lax.axis_size("context")
    cap = 2 * tok_rows // experts
    slots = experts * cap
    chans = w_inner.shape[3]
    heads = w_step.shape[2]
    nstate = w_state.shape[2] // 2
    chips = shards // 2
    far_count = shards - 2

    here = lax.axis_index("context").astype(jnp.int32)
    blocks = jnp.arange(shards, dtype=jnp.int32)
    order = 2 * ((here // 2 - blocks // 2) % chips) + ((here % 2) ^ (blocks % 2))
    groups = 2 * ((blocks // 2 - here // 2) % chips) + ((here % 2) ^ (blocks % 2))
    block_at = 2 * ((here // 2 - blocks // 2) % chips) + ((here % 2) ^ (blocks % 2))
    info = jnp.concatenate([here[None], block_at, order, groups])
    ids = route.reshape(shards, 1, tok_rows)
    swap = [(c, c ^ 1) for c in range(shards)]

    def hop(k):
        return [(c, ((c // 2 + k) % chips) * 2 + c % 2) for c in range(shards)]

    def permute(value, pairs):
        return lax.ppermute(value, "context", pairs)

    def spread(value):
        made = [value, permute(value, swap)]
        for k in range(1, chips):
            arrived = permute(value, hop(k))
            made += [arrived, permute(arrived, swap)]
        return made

    def exchange(value):
        return lax.all_to_all(value, "expert", split_axis=0, concat_axis=0, tiled=True)

    w_flat = w_inner[0].reshape(width, 2 * chans)

    outgoing = call(
        functools.partial(dispatch_kernel, experts, cap),
        [info, ids, tokens[0]],
        [shape(slots, width)],
        flops=2 * slots * tok_rows * width,
    )[0]
    own = exchange(outgoing.reshape(experts, cap, width)).reshape(slots, width)
    steps = spread(tie(w_step[0].T, outgoing))
    own = tie(own, w_flat, *steps)
    swapped = permute(own, swap)
    near = call(
        functools.partial(project_kernel, 2, experts, cap, chans),
        [info, own, swapped, w_state[0], *steps],
        [shape(experts, 2, cap, chans + LANES)],
        streamed=[w_flat],
        scratch=held_weight(width, chans, 256),
        flops=4 * slots * width * (chans + LANES),
    )[0]
    distant = []
    for k in range(1, chips):
        arrived = permute(own, hop(k))
        distant += [arrived, permute(tie(arrived, near), swap)]
    far = call(
        functools.partial(project_kernel, far_count, experts, cap, chans),
        [info, *distant],
        [shape(experts, far_count, cap, chans)],
        streamed=[w_flat],
        scratch=held_weight(width, chans, 256),
        flops=2 * far_count * slots * width * chans,
    )[0]
    near_back = exchange(near)
    far_back = exchange(far)

    side = call(
        functools.partial(side_kernel, experts, cap, chans),
        [info, ids, near_back],
        [shape(tok_rows, 2 * LANES)],
        after=[far],
        flops=2 * slots * tok_rows * 2 * LANES,
    )[0]
    sides = jnp.stack(spread(side))

    def padded_heads(row):
        return jnp.pad(row, (0, LANES - heads))[None, :]

    head_rows = jnp.concatenate(
        [padded_heads(step_bias), padded_heads(-jnp.exp(decay_log)), jnp.zeros((6, LANES), F32)]
    )
    chan_rows = jnp.concatenate(
        [conv_weight, conv_bias[None, :], jnp.repeat(skip_gain, HEAD_DIM)[None, :]]
    )
    chan_rows = jnp.pad(chan_rows, ((0, 2), (0, 0)))
    def gates(rows):
        return call(
            functools.partial(gate_kernel, len(rows), chans),
            [info, *rows],
            [shape(slots, chans)] * len(rows),
            streamed=[w_flat],
            scratch=held_weight(width, chans, 256),
            after=[far],
            flops=2 * len(rows) * slots * width * chans,
        )

    gate_far = gates(distant)
    gate_near = gates([own, swapped])
    cfg = (experts, cap, tok_rows, nstate, chans, heads)
    near_out, far_out = call(
        functools.partial(scan_kernel, cfg),
        [info, ids, sides, head_rows, chan_rows, near_back, far_back],
        [shape(experts, 2, cap, chans), shape(experts, far_count, cap, chans)],
        after=[gate_far[0], gate_near[0]],
        scratch=[
            pltpu.VMEM((8 + shards * tok_rows, chans), F32),
            pltpu.VMEM((shards * tok_rows, chans), BF16),
        ],
        flops=2 * shards * tok_rows * chans * (2 * slots + 2 * nstate + 2 * tok_rows + 768),
        exps=shards * tok_rows * tok_rows * heads,
    )
    far_ret = exchange(far_out)
    near_ret = exchange(near_out)

    def outputs(scanned, gate, places, after=()):
        return call(
            functools.partial(output_kernel, places),
            [info, scanned, *(gate[at] for at in places)],
            [shape(slots, width)] * len(places),
            streamed=[w_out[0]],
            after=after,
            scratch=held_weight(chans, width, 512),
            flops=2 * len(places) * slots * width * chans,
        )

    parts_other = outputs(far_ret, gate_far, range(1, far_count, 2))
    parts_other = [permute(part, swap) for part in parts_other]
    parts_mine = outputs(far_ret, gate_far, range(0, far_count, 2))
    hopped = []
    for k in range(1, chips):
        pair = parts_mine[k - 1].astype(F32) + parts_other[k - 1].astype(F32)
        hopped.append(permute(pair.astype(BF16), hop(chips - k)))
    part_swap = outputs(near_ret, gate_near, [1])[0]
    part_own = outputs(near_ret, gate_near, [0], hopped)[0]
    summed = call(
        sum_kernel, [info, part_own, permute(part_swap, swap), *hopped], [shape(slots, width)]
    )[0]
    returned = exchange(summed.reshape(experts, cap, width)).reshape(slots, width)
    result = call(
        functools.partial(collect_kernel, experts, cap),
        [info, ids, returned],
        [shape(tok_rows, width)],
        flops=2 * slots * tok_rows * width,
    )[0]
    return result[None]


def solution(mesh):
    in_specs = (
        P("expert", "context", None),
        P("expert", None, None),
        P("expert", None, None, "context"),
        P("expert", None, None),
        P("expert", None, "context"),
        P("context"),
        P("context"),
        P("context"),
        P(None, "context"),
        P("context"),
        P("expert", "context", None),
    )
    out_specs = P("expert", "context", None)
    return jax.shard_map(
        per_device, mesh=mesh, in_specs=in_specs, out_specs=out_specs, check_vma=False
    )
```

time: 235 us -> 237 us (level)
  Pallas kernels: 36.3 us -> 49.9 us
  waiting for transfers between devices: 66.8 us -> 61.7 us
  local copies, waits for them, and re-layouts: 38.8 us -> 36.1 us
    ppermute x12, waiting for transfers between devices: 33 us -> 18.8 us  [permute(): return lax.ppermute(value, 'context', pairs)]
    pallas_call x12 -> x13, Pallas kernels: 36.3 us -> 49.9 us  [call(): pl.pallas_call(body, out_shape=outputs, in_specs=[ANY] * len(streamed) +...]
    all_to_all x4, waiting for transfers between devices: 33.8 us -> 43 us  [exchange(): lax.all_to_all(value, 'expert', split_axis=0, concat_axis=0, tiled=True)]
    unnamed x67 -> x71, local copies, waits for them, and re-layouts: 37.4 us -> 35.9 us
  transfers between devices with their start and end apart: 16 -> 16, of which waited for: 10 -> 9; matrix products, arithmetic and copies ran while one was open for 7% -> 5% of each run, Pallas kernels for 9% -> 15%
where the time goes in v2:
time: 237 us; the launch traced here: 236 us
  waiting for transfers between devices  61.7 us (26%)
  blocking collectives  60.5 us (26%)
  Pallas kernels  49.9 us (21%)
  local copies, waits for them, and re-layouts  36.1 us (15%)
  starting transfers between devices  25.9 us (11%)
    all_to_all x2, blocking collectives, exchange(): lax.all_to_all(value, 'expert', split_axis=0, concat_axis=0, tiled=True)  60.5 us
    pallas_call x13, Pallas kernels, call(): pl.pallas_call(body, out_shape=outputs, in_specs=[ANY] * len(streamed) +...  49.9 us
    all_to_all x4, waiting for transfers between devices, exchange(): lax.all_to_all(value, 'expert', split_axis=0, concat_axis=0, tiled=True)  43 us
    unnamed x71, local copies, waits for them, and re-layouts  35.9 us
    all_to_all x4, starting transfers between devices, exchange(): lax.all_to_all(value, 'expert', split_axis=0, concat_axis=0, tiled=True)  19.1 us
    ppermute x12, waiting for transfers between devices, permute(): return lax.ppermute(value, 'context', pairs)  18.8 us
    ppermute x12, starting transfers between devices, permute(): return lax.ppermute(value, 'context', pairs)  6.86 us
  transfers between devices with their start and end apart: 16, of which 9 were waited for; matrix products, arithmetic and copies ran while one was open for 5% of the time, Pallas kernels for 15%

profile of v2, /device:TPU:0, one launch (start us, length us, event | category | flops | bytes accessed | tf_op | source)
XLA Modules:
  0.0 236.2 jit_solution(12527210477371578404)
XLA Ops:
  5.4 7.3 %all-to-all-start = ((bf16[8,32,2048]{2,1,0:T(8,128)(2,1)}), bf16[8,32,2048]{2,1,0:T(8,128)(2,1)S(1)}, u32[]{:S(2)}, u32[]{:S(2)}) async-start(bf16[8,32,2048]{2,1,0:T(8,128)(2,1)} %bitcast.4), calls=%async_computation | async-start | bytes 2097152 | tf_op jit(solution)/shard_map/all_to_all | solution.py:322
  17.2 10.2 %copy.15 = bf16[256,8,2,1024]{3,1,2,0:T(8,128)(2,1)} copy(bf16[256,8,2,1024]{3,2,1,0:T(2,128)(2,1)} %bitcast.45) | data formatting | bytes 16777216
  27.5 11.0 %all-to-all-done = bf16[8,32,2048]{2,1,0:T(8,128)(2,1)S(1)} async-done(((bf16[8,32,2048]{2,1,0:T(8,128)(2,1)}), bf16[8,32,2048]{2,1,0:T(8,128)(2,1)S(1)}, u32[]{:S(2)}, u32[]{:S(2)}) %all-to-all-start) | async-done | bytes 1048608 | tf_op jit(solution)/shard_map/all_to_all | solution.py:322
  48.6 5.9 %shard_map.112.refs_1_ = bf16[8,2,32,1152]{3,2,1,0:T(8,128)(2,1)} custom-call(bf16[2048,2048]{1,0:T(8,128)(2,1)S(1)} %bitcast.26, s32[13]{0:T(128)S(1)} %pad_add_fusion.refs_0_.refs_1_, bf16[256,2048]{1,0:T(8,128)(2,1)S(1)} %copy-done.7, bf16[256,2048]{1,0:T(8,128)(2,1)S(1)} %collective-permute-done.3.refs_3_, bf16[2048,128]{1,0:T(8,128)(2,1)S(1)} %bitcast.39, ...), custom_call_target="tpu_custom_call" | custom-call | flops 2415919104 | bytes 12451840 | tf_op jit(solution)/shard_map/pallas_call | solution.py:53
  55.5 3.6 %all-to-all-start.1 = ((bf16[8,2,32,1152]{3,2,1,0:T(8,128)(2,1)}), bf16[8,2,32,1152]{3,2,1,0:T(8,128)(2,1)S(1)}, u32[]{:S(2)}, u32[]{:S(2)}) async-start(bf16[8,2,32,1152]{3,2,1,0:T(8,128)(2,1)} %shard_map.112.refs_1_), calls=%async_computation.1 | async-start | bytes 2359296 | tf_op jit(solution)/shard_map/all_to_all | solution.py:322
  59.1 6.1 %collective-permute-done.4.refs_2_ = bf16[256,2048]{1,0:T(8,128)(2,1)S(1)} collective-permute-done((bf16[256,2048]{1,0:T(8,128)(2,1)}, bf16[256,2048]{1,0:T(8,128)(2,1)S(1)}, u32[]{:S(2)}, u32[]{:S(2)}) %collective-permute-start.4) | collective-permute-done | bytes 1048608 | tf_op jit(solution)/shard_map/ppermute | solution.py:312
  69.0 3.4 %copy-done.1 = bf16[256,8,2,1024]{3,1,2,0:T(8,128)(2,1)S(1)} copy-done((bf16[256,8,2,1024]{3,1,2,0:T(8,128)(2,1)S(1)}, bf16[256,8,2,1024]{3,1,2,0:T(8,128)(2,1)}, u32[]{:S(2)}) %copy-start.1) | copy-done | bytes 8388632
  72.4 5.2 %shard_map.114.refs_3_.refs_4_ = bf16[8,2,32,1024]{3,2,1,0:T(8,128)(2,1)} custom-call(bf16[2048,2048]{1,0:T(8,128)(2,1)S(1)} %bitcast.27, s32[13]{0:T(128)S(1)} %pad_add_fusion.refs_0_.refs_1_, bf16[256,2048]{1,0:T(8,128)(2,1)S(1)} %collective-permute-done.4.refs_2_, bf16[256,2048]{1,0:T(8,128)(2,1)S(1)} %collective-permute-done.5.refs_3_), custom_call_target="tpu_custom_call" | custom-call | flops 2147483648 | bytes 11534336 | tf_op jit(solution)/shard_map/pallas_call | solution.py:53
  78.7 9.4 %all-to-all-done.1.refs_2_.refs_5_ = bf16[8,2,32,1152]{3,2,1,0:T(8,128)(2,1)S(1)} async-done(((bf16[8,2,32,1152]{3,2,1,0:T(8,128)(2,1)}), bf16[8,2,32,1152]{3,2,1,0:T(8,128)(2,1)S(1)}, u32[]{:S(2)}, u32[]{:S(2)}) %all-to-all-start.1) | async-done | bytes 1179680 | tf_op jit(solution)/shard_map/all_to_all | solution.py:322
  88.1 4.4 %all-to-all-start.2 = ((bf16[8,2,32,1024]{3,2,1,0:T(8,128)(2,1)}), bf16[8,2,32,1024]{3,2,1,0:T(8,128)(2,1)}, u32[]{:S(2)}, u32[]{:S(2)}) async-start(bf16[8,2,32,1024]{3,2,1,0:T(8,128)(2,1)} %shard_map.114.refs_3_.refs_4_), calls=%async_computation.2 | async-start | bytes 2097152 | tf_op jit(solution)/shard_map/all_to_all | solution.py:322
  95.4 3.4 %copy-done.2 = bf16[256,8,2,1024]{3,1,2,0:T(8,128)(2,1)S(1)} copy-done((bf16[256,8,2,1024]{3,1,2,0:T(8,128)(2,1)S(1)}, bf16[256,8,2,1024]{3,1,2,0:T(8,128)(2,1)}, u32[]{:S(2)}) %copy-start.2) | copy-done | bytes 8388632
  98.8 4.2 %shard_map.117 = (bf16[256,1024]{1,0:T(8,128)(2,1)S(1)}, bf16[256,1024]{1,0:T(8,128)(2,1)S(1)}) custom-call(bf16[2048,2048]{1,0:T(8,128)(2,1)S(1)} %bitcast.28, s32[13]{0:T(128)S(1)} %pad_add_fusion.refs_0_.refs_1_, bf16[256,2048]{1,0:T(8,128)(2,1)S(1)} %copy-done.8, bf16[256,2048]{1,0:T(8,128)(2,1)S(1)} %copy-done.10, ...), custom_call_target="tpu_custom_call" | custom-call | flops 2147483648 | bytes 11534336 | tf_op jit(solution)/shard_map/pallas_call | solution.py:53
  103.7 4.2 %shard_map.116 = (bf16[256,1024]{1,0:T(8,128)(2,1)S(1)}, bf16[256,1024]{1,0:T(8,128)(2,1)S(1)}) custom-call(bf16[2048,2048]{1,0:T(8,128)(2,1)S(1)} %bitcast.29, s32[13]{0:T(128)S(1)} %pad_add_fusion.refs_0_.refs_1_, bf16[256,2048]{1,0:T(8,128)(2,1)S(1)} %collective-permute-done.4.refs_2_, bf16[256,2048]{1,0:T(8,128)(2,1)S(1)} %copy-done.12, ...), custom_call_target="tpu_custom_call" | custom-call | flops 2147483648 | bytes 11534336 | tf_op jit(solution)/shard_map/pallas_call | solution.py:53
  108.0 9.8 %all-to-all-done.2.refs_6_ = bf16[8,2,32,1024]{3,2,1,0:T(8,128)(2,1)} async-done(((bf16[8,2,32,1024]{3,2,1,0:T(8,128)(2,1)}), bf16[8,2,32,1024]{3,2,1,0:T(8,128)(2,1)}, u32[]{:S(2)}, u32[]{:S(2)}) %all-to-all-start.2) | async-done | bytes 1048608 | tf_op jit(solution)/shard_map/all_to_all | solution.py:322
  118.9 9.4 %shard_map.118 = (bf16[8,2,32,1024]{3,2,1,0:T(8,128)(2,1)}, bf16[8,2,32,1024]{3,2,1,0:T(8,128)(2,1)S(1)}) custom-call(s32[13]{0:T(128)S(1)} %pad_add_fusion.refs_0_.refs_1_, s32[4,1,128]{2,1,0:T(1,128)S(1)} %bitcast.43, bf16[4,128,256]{2,1,0:T(8,128)(2,1)S(1)} %pad_maximum_fusion.refs_2_, f32[8,128]{1,0:T(8,128)S(1)} %maximum_maximum_fusion.refs_3_, ...), custom_call_target="tpu_custom_call" | custom-call | flops 1744830464 | bytes 4606976 | tf_op jit(solution)/shard_map/pallas_call | solution.py:53
  128.2 29.2 %all_to_all.30.refs_2_ = bf16[8,2,32,1024]{3,2,1,0:T(8,128)(2,1)S(1)} all-to-all(bf16[8,2,32,1024]{3,2,1,0:T(8,128)(2,1)S(1)} %get-tuple-element.14), channel_id=1, replica_groups=mesh['expert'=8,'context'=4] {'expert'}, dimensions={0} | all-to-all | bytes 2097152 | tf_op jit(solution)/shard_map/all_to_all | solution.py:322
  157.5 3.8 %all-to-all-start.3 = ((bf16[8,2,32,1024]{3,2,1,0:T(8,128)(2,1)}), bf16[8,2,32,1024]{3,2,1,0:T(8,128)(2,1)S(1)}, u32[]{:S(2)}, u32[]{:S(2)}) async-start(bf16[8,2,32,1024]{3,2,1,0:T(8,128)(2,1)} %get-tuple-element.13), calls=%async_computation.3 | async-start | bytes 2097152 | tf_op jit(solution)/shard_map/all_to_all | solution.py:322
  163.5 3.8 %shard_map.120 = bf16[256,2048]{1,0:T(8,128)(2,1)S(1)} custom-call(bf16[1024,2048]{1,0:T(8,128)(2,1)S(1)} %bitcast.30, s32[13]{0:T(128)S(1)} %pad_add_fusion.refs_0_.refs_1_, bf16[8,2,32,1024]{3,2,1,0:T(8,128)(2,1)S(1)} %all_to_all.30.refs_2_, bf16[256,1024]{1,0:T(8,128)(2,1)S(1)} %get-tuple-element.15.refs_3_), custom_call_target="tpu_custom_call" | custom-call | flops 1073741824 | bytes 6815744 | tf_op jit(solution)/shard_map/pallas_call | solution.py:53
  167.3 3.8 %shard_map.119 = bf16[256,2048]{1,0:T(8,128)(2,1)S(1)} custom-call(bf16[1024,2048]{1,0:T(8,128)(2,1)S(1)} %bitcast.31, s32[13]{0:T(128)S(1)} %pad_add_fusion.refs_0_.refs_1_, bf16[8,2,32,1024]{3,2,1,0:T(8,128)(2,1)S(1)} %all_to_all.30.refs_2_, bf16[256,1024]{1,0:T(8,128)(2,1)S(1)} %get-tuple-element.11.refs_7_.refs_3_), custom_call_target="tpu_custom_call" | custom-call | flops 1073741824 | bytes 6815744 | tf_op jit(solution)/shard_map/pallas_call | solution.py:53
  174.0 12.7 %all-to-all-done.3.refs_2_ = bf16[8,2,32,1024]{3,2,1,0:T(8,128)(2,1)S(1)} async-done(((bf16[8,2,32,1024]{3,2,1,0:T(8,128)(2,1)}), bf16[8,2,32,1024]{3,2,1,0:T(8,128)(2,1)S(1)}, u32[]{:S(2)}, u32[]{:S(2)}) %all-to-all-start.3) | async-done | bytes 1048608 | tf_op jit(solution)/shard_map/all_to_all | solution.py:322
  189.0 3.8 %shard_map.122 = bf16[256,2048]{1,0:T(8,128)(2,1)S(1)} custom-call(bf16[1024,2048]{1,0:T(8,128)(2,1)S(1)} %bitcast.32, s32[13]{0:T(128)S(1)} %pad_add_fusion.refs_0_.refs_1_, bf16[8,2,32,1024]{3,2,1,0:T(8,128)(2,1)S(1)} %all-to-all-done.3.refs_2_, bf16[256,1024]{1,0:T(8,128)(2,1)S(1)} %copy-done.20), custom_call_target="tpu_custom_call" | custom-call | flops 1073741824 | bytes 6815744 | tf_op jit(solution)/shard_map/pallas_call | solution.py:53
  192.8 5.5 %collective-permute-done.10.refs_4_.refs_3_ = bf16[256,2048]{1,0:T(8,128)(2,1)S(1)} collective-permute-done((bf16[256,2048]{1,0:T(8,128)(2,1)}, bf16[256,2048]{1,0:T(8,128)(2,1)S(1)}, u32[]{:S(2)}, u32[]{:S(2)}) %collective-permute-start.10) | collective-permute-done | bytes 1048608 | tf_op jit(solution)/shard_map/ppermute | solution.py:312
  198.3 3.8 %shard_map.121.refs_1_ = bf16[256,2048]{1,0:T(8,128)(2,1)S(1)} custom-call(bf16[1024,2048]{1,0:T(8,128)(2,1)S(1)} %bitcast.33, s32[13]{0:T(128)S(1)} %pad_add_fusion.refs_0_.refs_1_, bf16[8,2,32,1024]{3,2,1,0:T(8,128)(2,1)S(1)} %all-to-all-done.3.refs_2_, bf16[256,1024]{1,0:T(8,128)(2,1)S(1)} %copy-done.18, ...), custom_call_target="tpu_custom_call" | custom-call | flops 1073741824 | bytes 6815744 | tf_op jit(solution)/shard_map/pallas_call | solution.py:53
  203.0 31.3 %all_to_all.31 = bf16[8,32,2048]{2,1,0:T(8,128)(2,1)S(1)} all-to-all(bf16[8,32,2048]{2,1,0:T(8,128)(2,1)S(1)} %bitcast.35), channel_id=1, replica_groups=mesh['expert'=8,'context'=4] {'expert'}, dimensions={0} | all-to-all | bytes 2097152 | tf_op jit(solution)/shard_map/all_to_all | solution.py:322
  (109 shorter events, 40.5 us)
Async XLA Ops:
  5.4 33.0 %all-to-all-start = ((bf16[8,32,2048]{2,1,0:T(8,128)(2,1)}), bf16[8,32,2048]{2,1,0:T(8,128)(2,1)S(1)}, u32[]{:S(2)}, u32[]{:S(2)}) async-start(bf16[8,32,2048]{2,1,0:T(8,128)(2,1)} %bitcast.4), calls=%async_computation | async-start | bytes 2097152 | tf_op jit(solution)/shard_map/all_to_all | solution.py:322
  12.6 4.5 %collective-permute-start.1 = (bf16[16,2048]{1,0:T(8,128)(2,1)}, bf16[16,2048]{1,0:T(8,128)(2,1)S(1)}, u32[]{:S(2)}, u32[]{:S(2)}) collective-permute-start(bf16[16,2048]{1,0:T(8,128)(2,1)} %shard_map.110.refs_2_.refs_5_), channel_id=1, source_target_pairs={{0,2},{1,3},{2,0},{3,1},{4,6},{5,7},{6,4},{7,5},{8,10},{9,11},{10,... | collective-permute-start | bytes 196616 | tf_op jit(solution)/shard_map/ppermute | solution.py:312
  14.2 13.2 %collective-permute-start = (bf16[16,2048]{1,0:T(8,128)(2,1)}, bf16[16,2048]{1,0:T(8,128)(2,1)S(1)}, u32[]{:S(2)}, u32[]{:S(2)}) collective-permute-start(bf16[16,2048]{1,0:T(8,128)(2,1)} %shard_map.110.refs_2_.refs_5_), channel_id=1, source_target_pairs={{0,1},{1,0},{2,3},{3,2},{4,5},{5,4},{6,7},{7,6},{8,9},{9,8},{10,11... | collective-permute-start | bytes 196616 | tf_op jit(solution)/shard_map/ppermute | solution.py:312
  17.2 10.3 %collective-permute-start.2 = (bf16[16,2048]{1,0:T(8,128)(2,1)S(1)}, bf16[16,2048]{1,0:T(8,128)(2,1)S(1)}, u32[]{:S(2)}, u32[]{:S(2)}) collective-permute-start(bf16[16,2048]{1,0:T(8,128)(2,1)S(1)} %collective-permute-done.1.refs_4_.refs_7_), channel_id=1, source_target_pairs={{0,1},{1,0},{2,3},{3,2},{4,5},{5,4},{6,7},{7,6},{8,9},{9,8},{10,11... | collective-permute-start | bytes 196616 | tf_op jit(solution)/shard_map/ppermute | solution.py:312
  39.4 2.9 %collective-permute-start.3 = (bf16[256,2048]{1,0:T(8,128)(2,1)}, bf16[256,2048]{1,0:T(8,128)(2,1)S(1)}, u32[]{:S(2)}, u32[]{:S(2)}) collective-permute-start(bf16[256,2048]{1,0:T(8,128)(2,1)} %shard_map.111.refs_2_), channel_id=1, source_target_pairs={{0,1},{1,0},{2,3},{3,2},{4,5},{5,4},{6,7},{7,6},{8,9},{9,8},{10,11... | collective-permute-start | bytes 3145736 | tf_op jit(solution)/shard_map/ppermute | solution.py:312
  39.4 25.8 %collective-permute-start.4 = (bf16[256,2048]{1,0:T(8,128)(2,1)}, bf16[256,2048]{1,0:T(8,128)(2,1)S(1)}, u32[]{:S(2)}, u32[]{:S(2)}) collective-permute-start(bf16[256,2048]{1,0:T(8,128)(2,1)} %shard_map.111.refs_2_), channel_id=1, source_target_pairs={{0,2},{1,3},{2,0},{3,1},{4,6},{5,7},{6,4},{7,5},{8,10},{9,11},{10,... | collective-permute-start | bytes 3145736 | tf_op jit(solution)/shard_map/ppermute | solution.py:312
  55.5 32.6 %all-to-all-start.1 = ((bf16[8,2,32,1152]{3,2,1,0:T(8,128)(2,1)}), bf16[8,2,32,1152]{3,2,1,0:T(8,128)(2,1)S(1)}, u32[]{:S(2)}, u32[]{:S(2)}) async-start(bf16[8,2,32,1152]{3,2,1,0:T(8,128)(2,1)} %shard_map.112.refs_1_), calls=%async_computation.1 | async-start | bytes 2359296 | tf_op jit(solution)/shard_map/all_to_all | solution.py:322
  66.2 2.9 %collective-permute-start.5 = (bf16[256,2048]{1,0:T(8,128)(2,1)}, bf16[256,2048]{1,0:T(8,128)(2,1)S(1)}, u32[]{:S(2)}, u32[]{:S(2)}) collective-permute-start(bf16[256,2048]{1,0:T(8,128)(2,1)} %shard_map.113), channel_id=1, source_target_pairs={{0,1},{1,0},{2,3},{3,2},{4,5},{5,4},{6,7},{7,6},{8,9},{9,8},{10,11... | collective-permute-start | bytes 3145736 | tf_op jit(solution)/shard_map/ppermute | solution.py:312
  78.6 13.9 %copy-start.31 = (f32[16]{0:T(128)S(1)}, f32[16]{0:T(128)}, u32[]{:S(2)}) copy-start(f32[16]{0:T(128)} %param.18) | copy-start | bytes 196
  78.7 14.1 %copy-start.33 = (f32[16]{0:T(128)S(1)}, f32[16]{0:T(128)}, u32[]{:S(2)}) copy-start(f32[16]{0:T(128)} %param.17) | copy-start | bytes 196
  78.7 14.1 %copy-start.32 = (f32[16]{0:T(128)S(1)}, f32[16]{0:T(128)}, u32[]{:S(2)}) copy-start(f32[16]{0:T(128)} %param.16) | copy-start | bytes 196
  78.7 14.2 %copy-start.29 = (f32[4,1024]{1,0:T(4,128)S(1)}, f32[4,1024]{1,0:T(4,128)}, u32[]{:S(2)}) copy-start(f32[4,1024]{1,0:T(4,128)} %param.19) | copy-start | bytes 49156
  78.7 14.2 %copy-start.30 = (f32[1024]{0:T(1024)S(1)}, f32[1024]{0:T(1024)}, u32[]{:S(2)}) copy-start(f32[1024]{0:T(1024)} %param.20) | copy-start | bytes 12292
  78.7 14.3 %copy-start.28 = (s32[1,512,1]{1,2,0:T(1,128)S(1)}, s32[1,512,1]{1,2,0:T(1,128)}, u32[]{:S(2)}) copy-start(s32[1,512,1]{1,2,0:T(1,128)} %param.12) | copy-start | bytes 6148
  78.7 16.7 %copy-start.8 = (bf16[256,2048]{1,0:T(8,128)(2,1)S(1)}, bf16[256,2048]{1,0:T(8,128)(2,1)}, u32[]{:S(2)}) copy-start(bf16[256,2048]{1,0:T(8,128)(2,1)} %shard_map.111.refs_2_) | copy-start | bytes 3145732
  88.1 29.7 %all-to-all-start.2 = ((bf16[8,2,32,1024]{3,2,1,0:T(8,128)(2,1)}), bf16[8,2,32,1024]{3,2,1,0:T(8,128)(2,1)}, u32[]{:S(2)}, u32[]{:S(2)}) async-start(bf16[8,2,32,1024]{3,2,1,0:T(8,128)(2,1)} %shard_map.114.refs_3_.refs_4_), calls=%async_computation.2 | async-start | bytes 2097152 | tf_op jit(solution)/shard_map/all_to_all | solution.py:322
  93.9 9.3 %collective-permute-start.7 = (bf16[128,256]{1,0:T(8,128)(2,1)S(1)}, bf16[128,256]{1,0:T(8,128)(2,1)S(1)}, u32[]{:S(2)}, u32[]{:S(2)}) collective-permute-start(bf16[128,256]{1,0:T(8,128)(2,1)S(1)} %shard_map.115), channel_id=1, source_target_pairs={{0,2},{1,3},{2,0},{3,1},{4,6},{5,7},{6,4},{7,5},{8,10},{9,11},{10,... | collective-permute-start | bytes 196616 | tf_op jit(solution)/shard_map/ppermute | solution.py:312
  103.1 4.8 %collective-permute-start.6 = (bf16[128,256]{1,0:T(8,128)(2,1)S(1)}, bf16[128,256]{1,0:T(8,128)(2,1)S(1)}, u32[]{:S(2)}, u32[]{:S(2)}) collective-permute-start(bf16[128,256]{1,0:T(8,128)(2,1)S(1)} %shard_map.115), channel_id=1, source_target_pairs={{0,1},{1,0},{2,3},{3,2},{4,5},{5,4},{6,7},{7,6},{8,9},{9,8},{10,11... | collective-permute-start | bytes 196616 | tf_op jit(solution)/shard_map/ppermute | solution.py:312
  103.2 4.8 %collective-permute-start.8 = (bf16[128,256]{1,0:T(8,128)(2,1)S(1)}, bf16[128,256]{1,0:T(8,128)(2,1)S(1)}, u32[]{:S(2)}, u32[]{:S(2)}) collective-permute-start(bf16[128,256]{1,0:T(8,128)(2,1)S(1)} %collective-permute-done.7), channel_id=1, source_target_pairs={{0,1},{1,0},{2,3},{3,2},{4,5},{5,4},{6,7},{7,6},{8,9},{9,8},{10,11... | collective-permute-start | bytes 196616 | tf_op jit(solution)/shard_map/ppermute | solution.py:312
  157.5 29.3 %all-to-all-start.3 = ((bf16[8,2,32,1024]{3,2,1,0:T(8,128)(2,1)}), bf16[8,2,32,1024]{3,2,1,0:T(8,128)(2,1)S(1)}, u32[]{:S(2)}, u32[]{:S(2)}) async-start(bf16[8,2,32,1024]{3,2,1,0:T(8,128)(2,1)} %get-tuple-element.13), calls=%async_computation.3 | async-start | bytes 2097152 | tf_op jit(solution)/shard_map/all_to_all | solution.py:322
  167.3 3.9 %collective-permute-start.9 = (bf16[256,2048]{1,0:T(8,128)(2,1)S(1)}, bf16[256,2048]{1,0:T(8,128)(2,1)S(1)}, u32[]{:S(2)}, u32[]{:S(2)}) collective-permute-start(bf16[256,2048]{1,0:T(8,128)(2,1)S(1)} %shard_map.120), channel_id=1, source_target_pairs={{0,1},{1,0},{2,3},{3,2},{4,5},{5,4},{6,7},{7,6},{8,9},{9,8},{10,11... | collective-permute-start | bytes 3145736 | tf_op jit(solution)/shard_map/ppermute | solution.py:312
  171.2 15.6 %copy-start.20 = (bf16[256,1024]{1,0:T(8,128)(2,1)S(1)}, bf16[256,1024]{1,0:T(8,128)(2,1)}, u32[]{:S(2)}) copy-start(bf16[256,1024]{1,0:T(8,128)(2,1)} %copy-done.19) | copy-start | bytes 1572868
  172.5 25.8 %collective-permute-start.10 = (bf16[256,2048]{1,0:T(8,128)(2,1)}, bf16[256,2048]{1,0:T(8,128)(2,1)S(1)}, u32[]{:S(2)}, u32[]{:S(2)}) collective-permute-start(bf16[256,2048]{1,0:T(8,128)(2,1)} %add_convert_fusion), channel_id=1, source_target_pairs={{0,2},{1,3},{2,0},{3,1},{4,6},{5,7},{6,4},{7,5},{8,10},{9,11},{10,... | collective-permute-start | bytes 3145736 | tf_op jit(solution)/shard_map/ppermute | solution.py:312
  192.8 9.4 %collective-permute-start.11 = (bf16[256,2048]{1,0:T(8,128)(2,1)S(1)}, bf16[256,2048]{1,0:T(8,128)(2,1)S(1)}, u32[]{:S(2)}, u32[]{:S(2)}) collective-permute-start(bf16[256,2048]{1,0:T(8,128)(2,1)S(1)} %shard_map.122), channel_id=1, source_target_pairs={{0,1},{1,0},{2,3},{3,2},{4,5},{5,4},{6,7},{7,6},{8,9},{9,8},{10,11... | collective-permute-start | bytes 3145736 | tf_op jit(solution)/shard_map/ppermute | solution.py:312
  (26 other events, 95.5 us)
